TPU v7x, 32 devices: a whole 2x2x4 slice. The times are simulated.
32 devices in a mesh: dom: 8 (over z, core), col: 4 (over y, x).
Axes of the slice: x: 2, y: 2, z: 4, core: 2. Of those that a mesh axis runs over, the one named last changes fastest.
Arguments:
- features: bfloat16 [768, 32768], P('col', 'dom'), may hold values from -6 to 6
- tiles: bfloat16 [512, 128, 128], P('dom'), may hold values from -0.3984375 to 0.3984375
- tile_src_part: int32 [512, 1], P('dom'), may hold values from 0 to 7; in each aligned block of 64 rows (0 to 63, 64 to 127, ...) at most 16 rows name the same one
- tile_src_block: int32 [512], P('dom'), may hold values from 0 to 31
- tile_dst_block: int32 [512], P('dom'), may hold values from 0 to 23
- tile_count: int32 [8], P('dom'), may hold values from 1 to 64, 256 in all
- prior_hops: bfloat16 [2, 768, 24576], P(None, 'col', 'dom'), may hold values from -6 to 6
- labels: int32 [24576], P('dom'), may hold values from 0 to 152
- batch_of: int32 [24576, 1], P('dom'), may hold values from 0 to 15; in each aligned block of 3072 rows (0 to 3071, 3072 to 6143, ...) at most 240 rows name the same one
- w1: bfloat16 [4, 768, 1024], P(None, 'col'), may hold values from -0.109375 to 0.109375
- w2: bfloat16 [1024, 153], P('col')
Outputs:
- propagated: bfloat16 [768, 24576], P('col', 'dom')
- w1_new: float32 [4, 768, 1024], P(None, 'col')
- w2_new: float32 [1024, 153], P('col')
Inputs may be any that keep to these rules, and one draw needn't show every extreme that they name: `tile_src_part`: in the tile slots of one part no source part is named more than 16 times. `batch_of`: among the destination rows of one part no minibatch is named more than 240 times.
All inputs are finite; a program needn't handle non-finite values. No bound on the sum of `tile_count` on one device may be relied on, other than what follows from the above.
Results may differ from a plain program's by a relative error of at most 0.025.
Values may be sent and summed in bfloat16 or wider, within the bound.
A program may use at most 128 MiB of HBM per device.

v0:
```python
import jax
import jax.numpy as jnp
from jax import lax
from jax.sharding import PartitionSpec as P

STEPS = 2


step_rate = 0.02


def slot_ranks(keys, count):
    member = (keys[:, None] == jnp.arange(count, dtype=jnp.int32)[None, :]).astype(jnp.int32)
    return jnp.sum((jnp.cumsum(member, axis=0) - 1) * member, axis=1)


def per_device(
    features,
    tiles,
    tile_src_part,
    tile_src_block,
    tile_dst_block,
    tile_count,
    prior_hops,
    labels,
    batch_of,
    w1,
    w2,
):
    ndom = lax.axis_size("dom")
    width, srows = features.shape
    tilecap, blk, _unused = tiles.shape
    sblk = srows // blk
    drows = prior_hops.shape[2]
    dblk = drows // blk
    hops = w1.shape[0]
    classes = w2.shape[1]
    blocks = features.reshape(width, sblk, blk)
    valid = (jnp.arange(tilecap, dtype=jnp.int32) < tile_count[0]).astype(jnp.float32)
    src_part = tile_src_part[:, 0]
    gblock = src_part * sblk + tile_src_block
    piece = lax.all_gather(blocks, "dom", axis=1, tiled=True)
    count = piece.shape[1]
    inside = (gblock >= 0) & (gblock < count)
    picked = jnp.take(piece, jnp.clip(gblock, 0, count - 1), axis=1)
    sources = jnp.where(inside[None, :, None], picked, jnp.zeros_like(picked))
    contrib = (
        jnp.einsum("dtk,tik->dti", sources, tiles, preferred_element_type=jnp.float32)
        * valid[None, :, None]
    )
    target = (tile_dst_block[:, None] == jnp.arange(dblk, dtype=jnp.int32)[None, :]).astype(
        jnp.float32
    )
    summed = jnp.einsum("dti,tb->dbi", contrib, target, precision=lax.Precision.HIGHEST)
    propagated = summed.reshape(width, drows).astype(jnp.bfloat16)
    inputs = jnp.stack([features[:, :drows], propagated, prior_hops[0], prior_hops[1]])
    flat = inputs.reshape(hops * width, drows)
    buckets = STEPS * ndom
    capm = max(2, (5 * drows + 4 * buckets - 1) // (4 * buckets))
    bucket = batch_of[:, 0]
    place = bucket % ndom * STEPS * capm + bucket // ndom * capm + slot_ranks(bucket, buckets)
    packed = jnp.zeros((hops * width, ndom * STEPS * capm), jnp.bfloat16).at[:, place].set(flat)
    tags = jnp.full((ndom * STEPS * capm,), -1, jnp.int32).at[place].set(labels)
    rows_in, tags_in = (
        lax.all_to_all(
            packed.reshape(hops * width, ndom, STEPS, capm),
            "dom",
            split_axis=1,
            concat_axis=1,
            tiled=True,
        ),
        lax.all_to_all(
            tags.reshape(1, ndom, STEPS, capm), "dom", split_axis=1, concat_axis=1, tiled=True
        ),
    )
    w1_master = w1.astype(jnp.float32)
    w2_master = w2.astype(jnp.float32)
    for step in range(STEPS):
        batch_x = rows_in[:, :, step, :].reshape(hops, width, ndom * capm)
        batch_label = tags_in[0, :, step, :].reshape(ndom * capm)
        member = (batch_label >= 0).astype(jnp.float32)
        w1_low = w1_master.astype(jnp.bfloat16)
        w2_low = w2_master.astype(jnp.bfloat16)
        partial_value = jnp.einsum(
            "hdr,hdj->rj", batch_x, w1_low, preferred_element_type=jnp.float32
        )
        zpart = lax.psum_scatter(
            partial_value.astype(jnp.bfloat16), "col", scatter_dimension=1, tiled=True
        ).astype(jnp.float32)
        hidden = jax.nn.silu(zpart).astype(jnp.bfloat16)
        logits = lax.psum(jnp.dot(hidden, w2_low, preferred_element_type=jnp.float32), "col")
        prob = jax.nn.softmax(logits, axis=-1)
        onehot = (batch_label[:, None] == jnp.arange(classes, dtype=jnp.int32)[None, :]).astype(
            jnp.float32
        )
        slope = ((prob - onehot) * member[:, None]).astype(jnp.bfloat16)
        grad2 = jnp.dot(hidden.T, slope, preferred_element_type=jnp.float32)
        back = jnp.dot(slope, w2_low.T, preferred_element_type=jnp.float32)
        sig = jax.nn.sigmoid(zpart)
        dz = (back * sig * (1.0 + zpart * (1.0 - sig))).astype(jnp.bfloat16)
        dz_full = lax.all_gather(dz, "col", axis=1, tiled=True)
        grad1 = jnp.einsum("hdr,rj->hdj", batch_x, dz_full, preferred_element_type=jnp.float32)
        grad1, grad2 = lax.psum((grad1, grad2), "dom")
        w1_master = w1_master - step_rate * grad1
        w2_master = w2_master - step_rate * grad2
    return (propagated, w1_master, w2_master)


def solution(mesh):
    in_specs = (
        P("col", "dom"),
        P("dom", None, None),
        P("dom", None),
        P("dom"),
        P("dom"),
        P("dom"),
        P(None, "col", "dom"),
        P("dom"),
        P("dom", None),
        P(None, "col", None),
        P("col", None),
    )
    out_specs = (P("col", "dom"), P(None, "col", None), P("col", None))
    return jax.shard_map(
        per_device, mesh=mesh, in_specs=in_specs, out_specs=out_specs, check_vma=False
    )
```

profile of v0, /device:TPU:0, one launch (start us, length us, event | category | flops | bytes accessed | tf_op | source)
XLA Modules:
  0.0 865.4 jit_solution(10000914187912176641)
XLA Ops:
  7.3 3.1 copy_bitcast_fusion
  11.1 4.6 reduce-window.6
  15.7 0.4 slice_reduce_fusion
  16.7 2.4 slice_bitcast_fusion
  19.1 110.8 %all-gather.4.cloned.1.call-done = bf16[192,256,128]{2,0,1:T(8,128)(2,1)} async-done(((bf16[192,32,128]{2,0,1:T(8,128)(2,1)}), bf16[192,256,128]{2,0,1:T(8,128)(2,1)}) %all-gather.4.cloned.1.call-update) | async-done | bytes 12582928 | tf_op jit(solution)/shard_map/all_gather | solution.py:42
  130.0 7.2 gather_fusion
  137.2 3.4 multiply_bitcast_fusion
  140.6 5.8 fusion.36
  146.4 1.4 convert_element_type.103
  147.8 3.8 pad_maximum_fusion
  151.7 6.6 copy.24
  158.3 18.3 %scatter_custom_fusion = bf16[768,3840]{0,1:T(8,128)(2,1)} fusion(s32[3072]{0:T(1024)S(1)} %bitcast.98, bf16[768,3072]{0,1:T(8,128)(2,1)} %copy.24, bf16[]{:T(256)} %constant.68.clone.1), kind=kCustom, calls=%fused_computation.9 | custom fusion | bytes 10616834 | tf_op jit(solution)/shard_map/scatter | solution.py:62
  176.6 134.3 %all_to_all.10 = bf16[768,8,2,240]{0,3,2,1:T(8,128)(2,1)S(1)} all-to-all(bf16[768,8,2,240]{0,3,2,1:T(8,128)(2,1)} %bitcast.88), channel_id=1, replica_groups=mesh['dom'=8,'col'=4] {'dom'}, dimensions={1} | all-to-all | bytes 11796480 | tf_op jit(solution)/shard_map/all_to_all | solution.py:65
  310.9 2.9 fusion.59
  313.8 5.0 copy.25
  318.8 6.5 reshape_squeeze.8
  325.3 6.7 bitcast_convert_fusion.1
  332.1 49.3 %reduce-scatter.3.cloned.1.call-done = bf16[1920,256]{1,0:T(8,128)(2,1)} async-done(((bf16[1920,1024]{1,0:T(8,128)(2,1)}), bf16[1920,256]{1,0:T(8,128)(2,1)}) %reduce-scatter.3.cloned.1.call-update) | async-done | bytes 983056 | tf_op jit(solution)/shard_map/reduce_scatter | solution.py:87
  381.4 1.8 fusion.25
  383.2 1.5 fusion.60
  384.8 12.0 %scatter_custom_fusion.1 = s32[3840]{0:T(1024)S(1)} fusion(s32[3072]{0:T(1024)S(1)} %bitcast.99, s32[3072]{0:T(1024)} %param.18, s32[]{:T(128)} %constant.74.clone.1), kind=kCustom, calls=%fused_computation.86 | custom fusion | bytes 15872 | tf_op jit(solution)/shard_map/scatter | solution.py:63
  396.8 10.0 %all_to_all.11 = s32[1,8,2,240]{3,2,0,1:T(2,128)S(1)} all-to-all(s32[1,8,2,240]{3,2,0,1:T(2,128)S(1)} %reshape.86), channel_id=1, replica_groups=mesh['dom'=8,'col'=4] {'dom'}, dimensions={1} | all-to-all | bytes 30720 | tf_op jit(solution)/shard_map/all_to_all | solution.py:72
  407.0 33.3 %all-reduce.7.cloned.1.call-done = f32[1920,153]{0,1:T(8,128)} async-done(((f32[1920,153]{0,1:T(8,128)}), f32[1920,153]{0,1:T(8,128)}) %all-reduce.7.cloned.1.call-update) | async-done | bytes 1175056 | tf_op jit(solution)/shard_map/psum | solution.py:91
  440.4 1.5 reduce_max.18
  441.8 1.5 fusion.39
  443.3 0.4 multiply_convert_fusion.1
  443.7 3.2 fusion.17
  447.2 1.0 fusion.61
  448.2 49.4 %all-gather.6.cloned.1.call-done = bf16[1920,1024]{1,0:T(8,128)(2,1)} async-done(((bf16[1920,256]{1,0:T(8,128)(2,1)}), bf16[1920,1024]{1,0:T(8,128)(2,1)}) %all-gather.6.cloned.1.call-update) | async-done | bytes 3932176 | tf_op jit(solution)/shard_map/all_gather | solution.py:101
  497.6 8.1 fusion.6
  505.8 5.0 copy.26
  510.8 6.6 reshape_squeeze.9
  517.4 69.2 %all-reduce.13.cloned.1.call-done = (f32[4,192,1024]{2,1,0:T(8,128)}, f32[256,153]{0,1:T(8,128)}) async-done(((f32[4,192,1024]{2,1,0:T(8,128)}, f32[256,153]{0,1:T(8,128)}), (f32[4,192,1024]{2,1,0:T(8,128)}, f32[256,153]{0,1:T(8,128)})) %all-reduce.13.cloned.1.call-update) | async-done | bytes 3302416 | tf_op jit(solution)/shard_map/psum | solution.py:103
  586.5 8.1 bitcast_convert_fusion
  594.7 50.4 %reduce-scatter.5.cloned.1.call-done = bf16[1920,256]{1,0:T(8,128)(2,1)} async-done(((bf16[1920,1024]{1,0:T(8,128)(2,1)}), bf16[1920,256]{1,0:T(8,128)(2,1)}) %reduce-scatter.5.cloned.1.call-update) | async-done | bytes 983056 | tf_op jit(solution)/shard_map/reduce_scatter | solution.py:87
  645.1 1.8 fusion.30
  646.9 1.5 fusion.57
  648.6 55.8 %all-reduce.9.cloned.1.call-done = f32[1920,153]{0,1:T(8,128)} async-done(((f32[1920,153]{0,1:T(8,128)}), f32[1920,153]{0,1:T(8,128)}) %all-reduce.9.cloned.1.call-update) | async-done | bytes 1175056 | tf_op jit(solution)/shard_map/psum | solution.py:91
  704.4 1.5 reduce_max.19
  705.8 1.5 fusion.40
  707.7 3.2 fusion.18
  711.2 1.0 fusion.62
  712.2 49.4 %all-gather.8.cloned.1.call-done = bf16[1920,1024]{1,0:T(8,128)(2,1)} async-done(((bf16[1920,256]{1,0:T(8,128)(2,1)}), bf16[1920,1024]{1,0:T(8,128)(2,1)}) %all-gather.8.cloned.1.call-update) | async-done | bytes 3932176 | tf_op jit(solution)/shard_map/all_gather | solution.py:101
  761.6 8.1 fusion.4
  769.7 1.2 copy.37
  771.0 79.6 %all-reduce.11.cloned.1.call-done = (f32[4,192,1024]{2,1,0:T(8,128)}, f32[256,153]{0,1:T(8,128)}) async-done(((f32[4,192,1024]{2,1,0:T(8,128)}, f32[256,153]{0,1:T(8,128)}), (f32[4,192,1024]{2,1,0:T(8,128)}, f32[256,153]{0,1:T(8,128)})) %all-reduce.11.cloned.1.call-update) | async-done | bytes 3302416 | tf_op jit(solution)/shard_map/psum | solution.py:103
  850.5 1.6 multiply_subtract_fusion.2
  852.2 6.3 multiply_subtract_fusion
  (66 shorter events, 2.3 us)
Async XLA Ops:
  7.2 130.0 %copy-start = (bf16[64,128,128]{2,1,0:T(8,128)(2,1)S(1)}, bf16[64,128,128]{2,1,0:T(8,128)(2,1)}, u32[]{:S(2)}) copy-start(bf16[64,128,128]{2,1,0:T(8,128)(2,1)} %param.12) | copy-start | bytes 6291460
  7.2 3.9 copy-start.13
  7.2 9.2 %copy-start.15 = (s32[64,1]{0,1:T(1,128)S(1)}, s32[64,1]{0,1:T(1,128)}, u32[]{:S(2)}) copy-start(s32[64,1]{0,1:T(1,128)} %param.13) | copy-start | bytes 772
  7.2 9.2 %copy-start.14 = (s32[64]{0:T(128)S(1)}, s32[64]{0:T(128)}, u32[]{:S(2)}) copy-start(s32[64]{0:T(128)} %param.14) | copy-start | bytes 772
  7.2 122.8 %all-gather.4.cloned.1.call-start = ((), (), s32[]{:S(2)}) async-start(), calls=%async_computation.4 | async-start | bytes 14155776 | tf_op jit(solution)/shard_map/all_gather | solution.py:42
  10.4 371.0 %reduce-scatter.3.cloned.1.call-start = ((), (), s32[]{:S(2)}) async-start(), calls=%async_computation.5 | async-start | bytes 4915200 | tf_op jit(solution)/shard_map/reduce_scatter | solution.py:87
  137.2 3.4 copy-start.16
  146.4 1.4 copy-start.8
  318.8 6.5 copy-start.9
  332.0 51.1 %copy-start.11 = (bf16[256,153]{0,1:T(8,128)(2,1)S(1)}, bf16[256,153]{0,1:T(8,128)(2,1)}, u32[]{:S(2)}) copy-start(bf16[256,153]{0,1:T(8,128)(2,1)} %param.21) | copy-start | bytes 235012
  332.1 108.3 %all-reduce.7.cloned.1.call-start = ((), (), s32[]{:S(2)}) async-start(), calls=%async_computation.6 | async-start | bytes 2457600 | tf_op jit(solution)/shard_map/psum | solution.py:91
  383.2 23.9 %copy-start.4 = (bf16[1920,256]{1,0:T(8,128)(2,1)}, bf16[1920,256]{1,0:T(8,128)(2,1)S(1)}, u32[]{:S(2)}) copy-start(bf16[1920,256]{1,0:T(8,128)(2,1)S(1)} %fusion.25) | copy-start | bytes 2949124
  384.7 112.9 %all-gather.6.cloned.1.call-start = ((), (), s32[]{:S(2)}) async-start(), calls=%async_computation.7 | async-start | bytes 4915200 | tf_op jit(solution)/shard_map/all_gather | solution.py:101
  440.4 2.9 copy-start.2
  443.7 3.5 copy-start.5
  446.9 139.6 %all-reduce.13.cloned.1.call-start = ((), (), s32[]{:S(2)}) async-start(), calls=%async_computation.12 | async-start | bytes 6619136 | tf_op jit(solution)/shard_map/psum | solution.py:103
  505.7 139.4 %reduce-scatter.5.cloned.1.call-start = ((), (), s32[]{:S(2)}) async-start(), calls=%async_computation.8 | async-start | bytes 4915200 | tf_op jit(solution)/shard_map/reduce_scatter | solution.py:87
  510.8 75.8 %copy-start.10 = (bf16[4,192,1024]{2,1,0:T(8,128)(2,1)S(1)}, bf16[4,192,1024]{2,1,0:T(8,128)(2,1)}, u32[]{:S(2)}) copy-start(bf16[4,192,1024]{2,1,0:T(8,128)(2,1)} %param.20) | copy-start | bytes 4718596
  594.6 52.3 %copy-start.12 = (f32[256,153]{0,1:T(8,128)S(1)}, f32[256,153]{0,1:T(8,128)}, u32[]{:S(2)}) copy-start(f32[256,153]{0,1:T(8,128)} %get-tuple-element.8) | copy-start | bytes 470020
  594.6 109.8 %all-reduce.9.cloned.1.call-start = ((), (), s32[]{:S(2)}) async-start(), calls=%async_computation.9 | async-start | bytes 2457600 | tf_op jit(solution)/shard_map/psum | solution.py:91
  646.9 1.7 copy-start.6
  648.4 113.2 %all-gather.8.cloned.1.call-start = ((), (), s32[]{:S(2)}) async-start(), calls=%async_computation.10 | async-start | bytes 4915200 | tf_op jit(solution)/shard_map/all_gather | solution.py:101
  704.4 2.9 copy-start.3
  707.7 3.5 copy-start.7
  710.9 139.6 %all-reduce.11.cloned.1.call-start = ((), (), s32[]{:S(2)}) async-start(), calls=%async_computation.11 | async-start | bytes 6619136 | tf_op jit(solution)/shard_map/psum | solution.py:103
  852.2 6.3 copy-start.1
Sparse Core Ops, SparseCore 0:
  10.5 119.4 all-gather.3
  332.2 49.1 reduce-scatter.2
  385.1 55.2 all-reduce.6
  447.0 50.5 all-gather.5
  505.9 80.6 all-reduce.12
  594.8 50.3 reduce-scatter.4
  649.1 55.1 all-reduce.8
  711.0 50.5 all-gather.7
  769.9 80.6 all-reduce.10
where the time goes:
time: 874 us; the launch traced here: 865 us
  waiting for transfers between devices  547 us (63%)
  blocking collectives  144 us (16%)
  local copies, waits for them, and re-layouts  79.1 us (9%)
  matrix products  51.6 us (6%)
  other arithmetic  26.9 us (3%)
  between operations  15.2 us (2%)
    psum x2, waiting for transfers between devices, per_device(): grad1, grad2 = lax.psum((grad1, grad2), 'dom')  149 us
    all_to_all x1, blocking collectives, per_device(): lax.all_to_all(packed.reshape(hops * width, ndom, STEPS, capm), 'dom', sp...  134 us
    all_gather x1, waiting for transfers between devices, per_device(): piece = lax.all_gather(blocks, 'dom', axis=1, tiled=True)  111 us
    reduce_scatter x2, waiting for transfers between devices, per_device(): lax.psum_scatter(partial_value.astype(jnp.bfloat16), 'col', scatter_dimen...  99.7 us
    all_gather x2, waiting for transfers between devices, per_device(): dz_full = lax.all_gather(dz, 'col', axis=1, tiled=True)  98.8 us
    psum x2, waiting for transfers between devices, per_device(): lax.psum(jnp.dot(hidden, w2_low, preferred_element_type=jnp.float32), 'col')  89.1 us
    scatter x1, local copies, waits for them, and re-layouts, per_device(): jnp.zeros((hops * width, ndom * STEPS * capm), jnp.bfloat16).at[:, place]  18.3 us
  transfers between devices with their start and end apart: 9, of which 9 were waited for; matrix products, arithmetic and copies ran while one was open for 4% of the time, Pallas kernels for 0%

commit v1 on v0

v1 whole, which is shorter than its diff:
```python
import jax
import jax.numpy as jnp
from jax import lax
from jax.sharding import PartitionSpec as P

STEPS = 2


step_rate = 0.02


def per_device(
    features,
    tiles,
    tile_src_part,
    tile_src_block,
    tile_dst_block,
    tile_count,
    prior_hops,
    labels,
    batch_of,
    w1,
    w2,
):
    ndom = lax.axis_size("dom")
    ncol = lax.axis_size("col")
    col = lax.axis_index("col")
    width, srows = features.shape
    tilecap, blk, _unused = tiles.shape
    sblk = srows // blk
    drows = prior_hops.shape[2]
    dblk = drows // blk
    hops = w1.shape[0]
    classes = w2.shape[1]
    hid = w1.shape[2]

    buckets = STEPS * ndom
    capm = (5 * drows + 4 * buckets - 1) // (4 * buckets)
    window = min(drows, ndom * capm)
    step_of = batch_of[:, 0] // ndom
    first = (step_of == 0).astype(jnp.int32)
    rank = jnp.cumsum(first)
    n_first = rank[drows - 1]
    index = jnp.arange(drows, dtype=jnp.int32)
    place = jnp.where(first == 1, rank - 1, n_first + index - rank)
    moves = (place[:, None] == index[None, :]).astype(jnp.bfloat16)

    blocks = features.reshape(width, sblk, blk)
    piece = lax.all_gather(blocks, "dom", axis=1, tiled=True)
    w2_master = lax.all_gather(w2, "col", axis=0, tiled=True).astype(jnp.float32)

    known = jnp.concatenate(
        [features[:, :drows], prior_hops[0], prior_hops[1]], axis=0
    )
    known = jnp.dot(known, moves, preferred_element_type=jnp.float32).astype(jnp.bfloat16)
    tags = jnp.dot(
        jnp.broadcast_to(labels.astype(jnp.bfloat16)[None, :], (8, drows)),
        moves,
        preferred_element_type=jnp.float32,
    )[0].astype(jnp.int32)

    valid = (jnp.arange(tilecap, dtype=jnp.int32) < tile_count[0]).astype(jnp.float32)
    gblock = tile_src_part[:, 0] * sblk + tile_src_block
    sources = jnp.take(piece, gblock, axis=1, mode="clip")
    contrib = (
        jnp.einsum("dtk,tik->dti", sources, tiles, preferred_element_type=jnp.float32)
        * valid[None, :, None]
    )
    target = (tile_dst_block[:, None] == jnp.arange(dblk, dtype=jnp.int32)[None, :]).astype(
        jnp.float32
    )
    summed = jnp.einsum("dti,tb->dbi", contrib, target, precision=lax.Precision.HIGHEST)
    propagated = summed.reshape(width, drows).astype(jnp.bfloat16)
    fresh = jnp.dot(propagated, moves, preferred_element_type=jnp.float32).astype(jnp.bfloat16)
    flat = jnp.concatenate([known[:width], fresh, known[width:]], axis=0)

    share = window // ncol
    w1_master = w1.reshape(hops * width, hid).astype(jnp.float32)
    for step in range(STEPS):
        start = 0 if step == 0 else drows - window
        batch_x = lax.slice_in_dim(flat, start, start + window, axis=1)
        spot = start + col * share + jnp.arange(share, dtype=jnp.int32)
        batch_label = lax.dynamic_slice_in_dim(tags, start + col * share, share)
        member = (spot < n_first) if step == 0 else (spot >= n_first)
        member = member.astype(jnp.float32)
        w1_low = w1_master.astype(jnp.bfloat16)
        w2_low = w2_master.astype(jnp.bfloat16)
        partial_value = jnp.einsum(
            "dr,dj->rj", batch_x, w1_low, preferred_element_type=jnp.float32
        ).astype(jnp.bfloat16)
        z = lax.psum_scatter(
            partial_value, "col", scatter_dimension=0, tiled=True
        ).astype(jnp.float32)
        hidden = jax.nn.silu(z).astype(jnp.bfloat16)
        logits = jnp.dot(hidden, w2_low, preferred_element_type=jnp.float32)
        prob = jax.nn.softmax(logits, axis=-1)
        onehot = (batch_label[:, None] == jnp.arange(classes, dtype=jnp.int32)[None, :]).astype(
            jnp.float32
        )
        slope = ((prob - onehot) * member[:, None]).astype(jnp.bfloat16)
        back = jnp.dot(slope, w2_low.T, preferred_element_type=jnp.float32)
        sig = jax.nn.sigmoid(z)
        dz = (back * sig * (1.0 + z * (1.0 - sig))).astype(jnp.bfloat16)
        dz_full = lax.all_gather(dz, "col", axis=0, tiled=True)
        grad2 = jnp.dot(hidden.T, slope, preferred_element_type=jnp.float32)
        grad2 = lax.psum(grad2.astype(jnp.bfloat16), ("dom", "col"))
        grad1 = jnp.dot(batch_x, dz_full, preferred_element_type=jnp.float32)
        grad1 = lax.psum(grad1.astype(jnp.bfloat16), "dom")
        w1_master = w1_master - step_rate * grad1.astype(jnp.float32)
        w2_master = w2_master - step_rate * grad2.astype(jnp.float32)
    own = hid // ncol
    w2_new = lax.dynamic_slice_in_dim(w2_master, col * own, own, axis=0)
    return (propagated, w1_master.reshape(hops, width, hid), w2_new)


def solution(mesh):
    in_specs = (
        P("col", "dom"),
        P("dom", None, None),
        P("dom", None),
        P("dom"),
        P("dom"),
        P("dom"),
        P(None, "col", "dom"),
        P("dom"),
        P("dom", None),
        P(None, "col", None),
        P("col", None),
    )
    out_specs = (P("col", "dom"), P(None, "col", None), P("col", None))
    return jax.shard_map(
        per_device, mesh=mesh, in_specs=in_specs, out_specs=out_specs, check_vma=False
    )
```

time: 874 us -> 808 us (0.924)
  blocking collectives: 144 us -> 15.5 us
  waiting for transfers between devices: 547 us -> 650 us
  local copies, waits for them, and re-layouts: 79.1 us -> 18.3 us
  matrix products: 51.6 us -> 87.2 us
  other arithmetic: 26.9 us -> 11.7 us
    all_to_all x2 -> x0, blocking collectives: 144 us -> none  [the longest x1 134 us: per_device(): lax.all_to_all(packed.reshape(hops * width, ndom, STEPS, capm), 'dom', sp...]
    psum x4, waiting for transfers between devices: 238 us -> 370 us  [the longest x2 245 us: per_device(): grad2 = lax.psum(grad2.astype(jnp.bfloat16), ('dom', 'col'))]
    dot_general x6 -> x9, matrix products: 34 us -> 71.3 us  [the longest x1 19 us: per_device(): jnp.dot(propagated, moves, preferred_element_type=jnp.float32)]
    scatter x2 -> x0, local copies, waits for them, and re-layouts: 30.3 us -> none  [the longest x1 18.3 us: per_device(): jnp.zeros((hops * width, ndom * STEPS * capm), jnp.bfloat16).at[:, place]]
    reduce_scatter x2, waiting for transfers between devices: 99.7 us -> 82.6 us  [per_device(): lax.psum_scatter(partial_value, 'col', scatter_dimension=0, tiled=True)]
    all_gather x0 -> x1, blocking collectives: none -> 15.5 us  [per_device(): lax.all_gather(w2, 'col', axis=0, tiled=True).astype(jnp.float32)]
    another operation x3 -> x1, local copies, waits for them, and re-layouts: 15.5 us -> 0.11 us  [the longest x2 13.1 us: per_device(): batch_x = rows_in[:, :, step, :].reshape(hops, width, ndom * capm)]
    all_gather x1, waiting for transfers between devices: 111 us -> 97.6 us  [per_device(): piece = lax.all_gather(blocks, 'dom', axis=1, tiled=True)]
  transfers between devices with their start and end apart: 9 -> 9, of which waited for: 9 -> 9; matrix products, arithmetic and copies ran while one was open for 4% -> 6% of each run, Pallas kernels for 0% -> 0%
where the time goes in v1:
time: 808 us; the launch traced here: 799 us
  waiting for transfers between devices  650 us (80%)
  matrix products  87.2 us (11%)
  local copies, waits for them, and re-layouts  18.3 us (2%)
  blocking collectives  15.5 us (2%)
  between operations  15.2 us (2%)
  other arithmetic  11.7 us (1%)
    psum x2, waiting for transfers between devices, per_device(): grad2 = lax.psum(grad2.astype(jnp.bfloat16), ('dom', 'col'))  245 us
    psum x2, waiting for transfers between devices, per_device(): grad1 = lax.psum(grad1.astype(jnp.bfloat16), 'dom')  125 us
    all_gather x2, waiting for transfers between devices, per_device(): dz_full = lax.all_gather(dz, 'col', axis=0, tiled=True)  99.6 us
    all_gather x1, waiting for transfers between devices, per_device(): piece = lax.all_gather(blocks, 'dom', axis=1, tiled=True)  97.6 us
    reduce_scatter x2, waiting for transfers between devices, per_device(): lax.psum_scatter(partial_value, 'col', scatter_dimension=0, tiled=True)  82.6 us
    dot_general x1, matrix products, per_device(): jnp.dot(propagated, moves, preferred_element_type=jnp.float32)  19 us
  transfers between devices with their start and end apart: 9, of which 9 were waited for; matrix products, arithmetic and copies ran while one was open for 6% of the time, Pallas kernels for 0%

profile of v1, /device:TPU:0, one launch (start us, length us, event | category | flops | bytes accessed | tf_op | source)
XLA Modules:
  0.0 798.7 jit_solution(11397367636504343364)
XLA Ops:
  7.2 3.1 copy_bitcast_fusion
  10.4 0.6 copy-done.8
  11.1 0.3 reduce-window.9
  11.5 0.1 slice_reduce_fusion
  11.7 0.6 slice.49
  12.4 0.7 compare_select_fusion
  13.1 3.3 slice_bitcast_fusion.1
  16.4 15.3 %fusion.8 = bf16[576,3072]{1,0:T(8,128)(2,1)} fusion(s32[3072]{0:T(1024)S(1)} %bitcast.58, bf16[192,3072]{1,0:T(8,128)(2,1)} %get-tuple-element.4, bf16[192,3072]{1,0:T(8,128)(2,1)} %get-tuple-element.3, bf16[192,3072]{1,0:T(8,128)(2,1)S(1)} %slice-done.2), kind=kOutput, calls=%fused_computation.12 | convolution fusion | flops 10893459456 | bytes 7090176 | tf_op jit(solution)/shard_map/dot_general | solution.py:55
  32.4 97.6 %all-gather.4.cloned.1.call-done = bf16[192,256,128]{2,0,1:T(8,128)(2,1)} async-done(((bf16[192,32,128]{2,0,1:T(8,128)(2,1)}), bf16[192,256,128]{2,0,1:T(8,128)(2,1)}) %all-gather.4.cloned.1.call-update) | async-done | bytes 12582928 | tf_op jit(solution)/shard_map/all_gather | solution.py:49
  130.0 7.2 gather_fusion
  137.2 3.6 multiply_bitcast_fusion
  140.8 5.8 fusion.49
  146.6 0.2 copy.26
  146.9 19.0 %fusion.9 = bf16[192,3072]{1,0:T(8,128)(2,1)S(1)} fusion(bf16[192,3072]{1,0:T(8,128)(2,1)S(1)} %bitcast.54, s32[3072]{0:T(1024)S(1)} %bitcast.59), kind=kOutput, calls=%fused_computation.15 | convolution fusion | flops 3633905664 | bytes 2371584 | tf_op jit(solution)/shard_map/dot_general | solution.py:74
  165.9 0.4 pad_maximum_fusion
  166.3 2.1 copy-done.2
  168.5 5.0 convolution_convert_fusion.1
  173.5 0.6 copy-done.9
  174.2 0.2 copy-done.7
  174.4 15.5 %all_gather.13 = bf16[1024,153]{0,1:T(8,128)(2,1)S(1)} all-gather(bf16[256,153]{0,1:T(8,128)(2,1)S(1)} %copy-done.7), channel_id=1, replica_groups=mesh['dom'=8,'col'=4] {'col'}, dimensions={0}, use_global_device_ids=true | all-gather | bytes 391680 | tf_op jit(solution)/shard_map/all_gather | solution.py:50
  189.8 0.6 fusion.65
  190.5 6.3 fusion.15
  196.8 0.1 constant_dynamic-slice_fusion
  196.9 27.8 %reduce-scatter.3.cloned.1.call-done = bf16[480,1024]{1,0:T(8,128)(2,1)} async-done(((bf16[1920,1024]{1,0:T(8,128)(2,1)}), bf16[480,1024]{1,0:T(8,128)(2,1)}) %reduce-scatter.3.cloned.1.call-update) | async-done | bytes 983056 | tf_op jit(solution)/shard_map/reduce_scatter | solution.py:91
  224.7 1.9 fusion.30
  226.6 0.5 fusion.71
  227.1 0.1 fusion.52
  227.2 1.9 fusion.33
  229.1 50.6 %all-gather.6.cloned.1.call-done = bf16[1920,1024]{1,0:T(8,128)(2,1)} async-done(((bf16[480,1024]{1,0:T(8,128)(2,1)}), bf16[1920,1024]{1,0:T(8,128)(2,1)}) %all-gather.6.cloned.1.call-update) | async-done | bytes 3932176 | tf_op jit(solution)/shard_map/all_gather | solution.py:104
  279.7 7.6 fusion.41
  287.3 1.1 convolution_convert_fusion.3
  288.5 0.3 reduce-scatter.5.cloned.1.call-start
  288.7 60.8 %all-reduce.5.cloned.1.call-done = bf16[768,1024]{1,0:T(8,128)(2,1)} async-done(((bf16[768,1024]{1,0:T(8,128)(2,1)}), bf16[768,1024]{1,0:T(8,128)(2,1)}) %all-reduce.5.cloned.1.call-update) | async-done | bytes 1572880 | tf_op jit(solution)/shard_map/psum | solution.py:108
  349.6 8.0 %convolution_convert_fusion = bf16[1920,1024]{1,0:T(8,128)(2,1)} fusion(bf16[768,3072]{1,0:T(8,128)(2,1)} %copy-done.2, bf16[768,1024]{1,0:T(8,128)(2,1)} %all-reduce.5.cloned.1.call-done, bf16[768,1024]{1,0:T(8,128)(2,1)} %bitcast.52), kind=kOutput, calls=%fused_computation.13 | convolution fusion | flops 3025797120 | bytes 10027008 | tf_op jit(solution)/shard_map/dr,dj->rj/dot_general | solution.py:88
  357.6 0.6 fusion.66
  358.3 121.0 %all-reduce.7.cloned.1.call-done = bf16[1024,153]{0,1:T(8,128)(2,1)} async-done(((bf16[1024,153]{0,1:T(8,128)(2,1)}), bf16[1024,153]{0,1:T(8,128)(2,1)}) %all-reduce.7.cloned.1.call-update) | async-done | bytes 313360 | tf_op jit(solution)/shard_map/psum | solution.py:106
  479.3 54.8 %reduce-scatter.5.cloned.1.call-done = bf16[480,1024]{1,0:T(8,128)(2,1)} async-done(((bf16[1920,1024]{1,0:T(8,128)(2,1)}), bf16[480,1024]{1,0:T(8,128)(2,1)}) %reduce-scatter.5.cloned.1.call-update) | async-done | bytes 983056 | tf_op jit(solution)/shard_map/reduce_scatter | solution.py:91
  534.1 2.1 fusion.72
  536.2 0.1 fusion.53
  536.3 2.0 fusion.40
  538.3 1.5 convolution_convert_fusion.2
  539.9 49.0 %all-gather.8.cloned.1.call-done = bf16[1920,1024]{1,0:T(8,128)(2,1)} async-done(((bf16[480,1024]{1,0:T(8,128)(2,1)}), bf16[1920,1024]{1,0:T(8,128)(2,1)}) %all-gather.8.cloned.1.call-update) | async-done | bytes 3932176 | tf_op jit(solution)/shard_map/all_gather | solution.py:104
  588.9 7.6 fusion.44
  596.5 0.1 multiply_subtract_fusion.2
  596.6 124.0 %all-reduce.11.cloned.1.call-done = bf16[1024,153]{0,1:T(8,128)(2,1)} async-done(((bf16[1024,153]{0,1:T(8,128)(2,1)}), bf16[1024,153]{0,1:T(8,128)(2,1)}) %all-reduce.11.cloned.1.call-update) | async-done | bytes 313360 | tf_op jit(solution)/shard_map/psum | solution.py:106
  720.6 1.7 dynamic-slice_subtract_fusion
  722.3 64.4 %all-reduce.9.cloned.1.call-done = bf16[768,1024]{1,0:T(8,128)(2,1)} async-done(((bf16[768,1024]{1,0:T(8,128)(2,1)}), bf16[768,1024]{1,0:T(8,128)(2,1)}) %all-reduce.9.cloned.1.call-update) | async-done | bytes 1572880 | tf_op jit(solution)/shard_map/psum | solution.py:108
  786.7 5.1 multiply_subtract_fusion
  (57 shorter events, 0.9 us)
Async XLA Ops:
  7.2 130.0 %copy-start = (bf16[64,128,128]{2,1,0:T(8,128)(2,1)S(1)}, bf16[64,128,128]{2,1,0:T(8,128)(2,1)}, u32[]{:S(2)}) copy-start(bf16[64,128,128]{2,1,0:T(8,128)(2,1)} %param.12) | copy-start | bytes 6291460
  7.2 122.8 %all-gather.4.cloned.1.call-start = ((), (), s32[]{:S(2)}) async-start(), calls=%async_computation.2 | async-start | bytes 14155776 | tf_op jit(solution)/shard_map/all_gather | solution.py:49
  10.4 0.7 copy-start.8
  10.4 214.4 %reduce-scatter.3.cloned.1.call-start = ((), (), s32[]{:S(2)}) async-start(), calls=%async_computation.3 | async-start | bytes 4915200 | tf_op jit(solution)/shard_map/reduce_scatter | solution.py:91
  13.1 3.3 slice-start.2
  31.6 0.7 copy-start.12
  31.7 0.7 copy-start.13
  137.2 3.6 copy-start.10
  146.8 19.1 %copy-start.4 = (bf16[24,8,24,128]{3,1,2,0:T(8,128)(2,1)}, bf16[24,8,24,128]{3,1,2,0:T(8,128)(2,1)S(1)}, u32[]{:S(2)}) copy-start(bf16[24,8,24,128]{3,1,2,0:T(8,128)(2,1)S(1)} %copy.26) | copy-start | bytes 3538948
  146.8 19.1 %slice-start = ((bf16[576,3072]{1,0:T(8,128)(2,1)}), bf16[384,3072]{1,0:T(8,128)(2,1)S(1)}, s32[]{:S(2)}) async-start(bf16[576,3072]{1,0:T(8,128)(2,1)} %fusion.8), calls=%async_computation.11 | async-start | bytes 4718592 | tf_op jit(solution)/shard_map/slice | solution.py:75
  146.8 19.1 %slice-start.1 = ((bf16[576,3072]{1,0:T(8,128)(2,1)}), bf16[192,3072]{1,0:T(8,128)(2,1)S(1)}, s32[]{:S(2)}) async-start(bf16[576,3072]{1,0:T(8,128)(2,1)} %fusion.8), calls=%async_computation.12 | async-start | bytes 2359296 | tf_op jit(solution)/shard_map/slice | solution.py:75
  165.9 2.5 copy-start.3
  166.3 2.1 copy-start.2
  173.5 0.7 copy-start.9
  173.5 0.9 copy-start.7
  173.5 106.2 %all-gather.6.cloned.1.call-start = ((), (), s32[]{:S(2)}) async-start(), calls=%async_computation.4 | async-start | bytes 4915200 | tf_op jit(solution)/shard_map/all_gather | solution.py:104
  224.7 2.4 copy-start.5
  229.0 120.5 %all-reduce.5.cloned.1.call-start = ((), (), s32[]{:S(2)}) async-start(), calls=%async_computation.5 | async-start | bytes 3145728 | tf_op jit(solution)/shard_map/psum | solution.py:108
  287.3 192.0 %all-reduce.7.cloned.1.call-start = ((), (), s32[]{:S(2)}) async-start(), calls=%async_computation.7 | async-start | bytes 655360 | tf_op jit(solution)/shard_map/psum | solution.py:106
  288.5 245.6 %reduce-scatter.5.cloned.1.call-start = ((), (), s32[]{:S(2)}) async-start(), calls=%async_computation.6 | async-start | bytes 4915200 | tf_op jit(solution)/shard_map/reduce_scatter | solution.py:91
  357.6 231.3 %all-gather.8.cloned.1.call-start = ((), (), s32[]{:S(2)}) async-start(), calls=%async_computation.8 | async-start | bytes 4915200 | tf_op jit(solution)/shard_map/all_gather | solution.py:104
  479.3 57.0 %copy-start.6 = (bf16[1024,153]{0,1:T(8,128)(2,1)S(1)}, bf16[1024,153]{0,1:T(8,128)(2,1)}, u32[]{:S(2)}) copy-start(bf16[1024,153]{0,1:T(8,128)(2,1)} %all-reduce.7.cloned.1.call-done) | copy-start | bytes 940036
  534.1 2.2 copy-start.11
  538.2 182.3 %all-reduce.11.cloned.1.call-start = ((), (), s32[]{:S(2)}) async-start(), calls=%async_computation.10 | async-start | bytes 655360 | tf_op jit(solution)/shard_map/psum | solution.py:106
  539.8 246.9 %all-reduce.9.cloned.1.call-start = ((), (), s32[]{:S(2)}) async-start(), calls=%async_computation.9 | async-start | bytes 3145728 | tf_op jit(solution)/shard_map/psum | solution.py:108
  720.6 71.2 %copy-start.1 = (bf16[64,128,128]{2,1,0:T(8,128)(2,1)S(1)}, bf16[64,128,128]{2,1,0:T(8,128)(2,1)}, u32[]{:S(2)}) copy-start(bf16[64,128,128]{2,1,0:T(8,128)(2,1)} %param.12) | copy-start | bytes 6291460
Sparse Core Ops, SparseCore 0:
  10.5 119.4 all-gather.3
  173.6 51.0 reduce-scatter.2
  229.2 50.4 all-gather.5
  287.4 62.0 all-reduce.4
  354.8 124.4 all-reduce.6
  482.5 51.5 reduce-scatter.4
  538.4 50.4 all-gather.7
  595.1 125.4 all-reduce.10
  723.5 63.1 all-reduce.8

commit v2 on v1

--- a/solution.py
+++ b/solution.py
@@ -4,6 +4,7 @@
 from jax.sharding import PartitionSpec as P
 
 STEPS = 2
+CHUNKS = 2
 
 
 step_rate = 0.02
@@ -45,19 +46,24 @@
     place = jnp.where(first == 1, rank - 1, n_first + index - rank)
     moves = (place[:, None] == index[None, :]).astype(jnp.bfloat16)
 
+    moves = lax.optimization_barrier(moves)
+
     blocks = features.reshape(width, sblk, blk)
     piece = lax.all_gather(blocks, "dom", axis=1, tiled=True)
-    w2_master = lax.all_gather(w2, "col", axis=0, tiled=True).astype(jnp.float32)
+    wide = -(-classes // 128) * 128
+    w2_own = w2.astype(jnp.float32)
 
+    def whole_w2(own):
+        low = jnp.pad(own.astype(jnp.bfloat16), ((0, 0), (0, wide - classes)))
+        return lax.all_gather(low, "col", axis=0, tiled=True)[:, :classes]
+
+    tag_row = jnp.broadcast_to(labels.astype(jnp.bfloat16)[None, :], (16, drows))
     known = jnp.concatenate(
-        [features[:, :drows], prior_hops[0], prior_hops[1]], axis=0
+        [features[:, :drows], prior_hops[0], prior_hops[1], tag_row], axis=0
     )
     known = jnp.dot(known, moves, preferred_element_type=jnp.float32).astype(jnp.bfloat16)
-    tags = jnp.dot(
-        jnp.broadcast_to(labels.astype(jnp.bfloat16)[None, :], (8, drows)),
-        moves,
-        preferred_element_type=jnp.float32,
-    )[0].astype(jnp.int32)
+    tags = known[(hops - 1) * width].astype(jnp.int32)
+    known = known[: (hops - 1) * width]
 
     valid = (jnp.arange(tilecap, dtype=jnp.int32) < tile_count[0]).astype(jnp.float32)
     gblock = tile_src_part[:, 0] * sblk + tile_src_block
@@ -72,25 +78,39 @@
     summed = jnp.einsum("dti,tb->dbi", contrib, target, precision=lax.Precision.HIGHEST)
     propagated = summed.reshape(width, drows).astype(jnp.bfloat16)
     fresh = jnp.dot(propagated, moves, preferred_element_type=jnp.float32).astype(jnp.bfloat16)
-    flat = jnp.concatenate([known[:width], fresh, known[width:]], axis=0)
 
     share = window // ncol
-    w1_master = w1.reshape(hops * width, hid).astype(jnp.float32)
+    span = hid // CHUNKS
+    w1_known = jnp.concatenate([w1[0], w1[2], w1[3]], axis=0).astype(jnp.float32)
+    w1_fresh = w1[1].astype(jnp.float32)
+    cuts = [slice(n * span, (n + 1) * span) for n in range(CHUNKS)]
+    w1_known = [w1_known[:, cut] for cut in cuts]
+    w1_fresh = [w1_fresh[:, cut] for cut in cuts]
+
+    def rows_by(x, w):
+        return jnp.einsum(
+            "dr,dj->rj", x, w.astype(jnp.bfloat16), preferred_element_type=jnp.float32
+        )
+
+    def after(value, earlier):
+        return value if earlier is None else lax.optimization_barrier((value, earlier))[0]
+
     for step in range(STEPS):
         start = 0 if step == 0 else drows - window
-        batch_x = lax.slice_in_dim(flat, start, start + window, axis=1)
+        x_known = lax.slice_in_dim(known, start, start + window, axis=1)
+        x_fresh = lax.slice_in_dim(fresh, start, start + window, axis=1)
         spot = start + col * share + jnp.arange(share, dtype=jnp.int32)
         batch_label = lax.dynamic_slice_in_dim(tags, start + col * share, share)
         member = (spot < n_first) if step == 0 else (spot >= n_first)
         member = member.astype(jnp.float32)
-        w1_low = w1_master.astype(jnp.bfloat16)
-        w2_low = w2_master.astype(jnp.bfloat16)
-        partial_value = jnp.einsum(
-            "dr,dj->rj", batch_x, w1_low, preferred_element_type=jnp.float32
-        ).astype(jnp.bfloat16)
-        z = lax.psum_scatter(
-            partial_value, "col", scatter_dimension=0, tiled=True
-        ).astype(jnp.float32)
+        w2_low = whole_w2(w2_own)
+        sums, last = [], None
+        for n in range(CHUNKS):
+            term = rows_by(x_known, w1_known[n]) + rows_by(x_fresh, w1_fresh[n])
+            term = after(term.astype(jnp.bfloat16), last)
+            last = lax.psum_scatter(term, "col", scatter_dimension=0, tiled=True)
+            sums.append(last)
+        z = jnp.concatenate(sums, axis=1).astype(jnp.float32)
         hidden = jax.nn.silu(z).astype(jnp.bfloat16)
         logits = jnp.dot(hidden, w2_low, preferred_element_type=jnp.float32)
         prob = jax.nn.softmax(logits, axis=-1)
@@ -101,16 +121,33 @@
         back = jnp.dot(slope, w2_low.T, preferred_element_type=jnp.float32)
         sig = jax.nn.sigmoid(z)
         dz = (back * sig * (1.0 + z * (1.0 - sig))).astype(jnp.bfloat16)
-        dz_full = lax.all_gather(dz, "col", axis=0, tiled=True)
         grad2 = jnp.dot(hidden.T, slope, preferred_element_type=jnp.float32)
-        grad2 = lax.psum(grad2.astype(jnp.bfloat16), ("dom", "col"))
-        grad1 = jnp.dot(batch_x, dz_full, preferred_element_type=jnp.float32)
-        grad1 = lax.psum(grad1.astype(jnp.bfloat16), "dom")
-        w1_master = w1_master - step_rate * grad1.astype(jnp.float32)
-        w2_master = w2_master - step_rate * grad2.astype(jnp.float32)
-    own = hid // ncol
-    w2_new = lax.dynamic_slice_in_dim(w2_master, col * own, own, axis=0)
-    return (propagated, w1_master.reshape(hops, width, hid), w2_new)
+        grad2 = jnp.pad(grad2.astype(jnp.bfloat16), ((0, 0), (0, wide - classes)))
+        grad2 = lax.psum_scatter(grad2, "col", scatter_dimension=0, tiled=True)
+        last, last_sum = None, None
+        for n in range(CHUNKS):
+            last = lax.all_gather(after(dz[:, cuts[n]], last), "col", axis=0, tiled=True)
+            both = jnp.concatenate(
+                [
+                    jnp.dot(x, last, preferred_element_type=jnp.float32).astype(jnp.bfloat16)
+                    for x in (x_known, x_fresh)
+                ],
+                axis=0,
+            )
+            both = after(both, last_sum)
+            if n == CHUNKS - 1:
+                both, grad2 = lax.psum((both, grad2), "dom")
+            else:
+                both = lax.psum(both, "dom")
+            last_sum = both
+            both = both.astype(jnp.float32)
+            w1_known[n] = w1_known[n] - step_rate * both[: (hops - 1) * width]
+            w1_fresh[n] = w1_fresh[n] - step_rate * both[(hops - 1) * width :]
+        w2_own = w2_own - step_rate * grad2[:, :classes].astype(jnp.float32)
+    w1_known = jnp.concatenate(w1_known, axis=1).reshape(hops - 1, width, hid)
+    w1_fresh = jnp.concatenate(w1_fresh, axis=1)[None]
+    w1_new = jnp.concatenate([w1_known[:1], w1_fresh, w1_known[1:]], axis=0)
+    return (propagated, w1_new, w2_own)
 
 
 def solution(mesh):

time: 808 us -> 776 us (0.960)
  waiting for transfers between devices: 650 us -> 582 us
  other arithmetic: 11.7 us -> 33 us
  blocking collectives: 15.5 us -> 33 us
    psum x4, waiting for transfers between devices: 370 us -> 222 us  [the longest x2 113 us: per_device(): both, grad2 = lax.psum((both, grad2), 'dom')]
    reduce_scatter x2 -> x6, waiting for transfers between devices: 82.6 us -> 147 us  [the longest x4 98.7 us: per_device(): last = lax.psum_scatter(term, 'col', scatter_dimension=0, tiled=True)]
    all_gather x2 -> x4, waiting for transfers between devices: 99.6 us -> 129 us  [per_device(): lax.all_gather(after(dz[:, cuts[n]], last), 'col', axis=0, tiled=True)]
    all_gather x1 -> x2, blocking collectives: 15.5 us -> 33 us  [whole_w2(): return lax.all_gather(low, 'col', axis=0, tiled=True)[:, :classes]]
    convert_element_type x1 -> x9, other arithmetic: 0.01 us -> 16.3 us  [the longest x1 8.31 us: per_device(): moves = (place[:, None] == index[None, :]).astype(jnp.bfloat16)]
    all_gather x1, waiting for transfers between devices: 97.6 us -> 82.2 us  [per_device(): piece = lax.all_gather(blocks, 'dom', axis=1, tiled=True)]
    dot_general x5 -> x16, matrix products: 34.4 us -> 46.8 us  [the longest x8 25.1 us: rows_by(): jnp.einsum('dr,dj->rj', x, w.astype(jnp.bfloat16), preferred_element_type...]
    dot_general x1, matrix products: 19 us -> 9.01 us  [per_device(): jnp.dot(propagated, moves, preferred_element_type=jnp.float32)]
  transfers between devices with their start and end apart: 9 -> 15, of which waited for: 9 -> 15; matrix products, arithmetic and copies ran while one was open for 6% -> 11% of each run, Pallas kernels for 0% -> 0%
where the time goes in v2:
time: 776 us; the launch traced here: 771 us
  waiting for transfers between devices  582 us (75%)
  matrix products  86.3 us (11%)
  other arithmetic  33 us (4%)
  blocking collectives  33 us (4%)
  local copies, waits for them, and re-layouts  19.9 us (3%)
  between operations  15.7 us (2%)
    all_gather x4, waiting for transfers between devices, per_device(): lax.all_gather(after(dz[:, cuts[n]], last), 'col', axis=0, tiled=True)  129 us
    psum x2, waiting for transfers between devices, per_device(): both, grad2 = lax.psum((both, grad2), 'dom')  113 us
    psum x2, waiting for transfers between devices, per_device(): both = lax.psum(both, 'dom')  109 us
    reduce_scatter x4, waiting for transfers between devices, per_device(): last = lax.psum_scatter(term, 'col', scatter_dimension=0, tiled=True)  98.7 us
    all_gather x1, waiting for transfers between devices, per_device(): piece = lax.all_gather(blocks, 'dom', axis=1, tiled=True)  82.2 us
    reduce_scatter x2, waiting for transfers between devices, per_device(): grad2 = lax.psum_scatter(grad2, 'col', scatter_dimension=0, tiled=True)  48.6 us
    all_gather x2, blocking collectives, whole_w2(): return lax.all_gather(low, 'col', axis=0, tiled=True)[:, :classes]  33 us
    dot_general x8, matrix products, rows_by(): jnp.einsum('dr,dj->rj', x, w.astype(jnp.bfloat16), preferred_element_type...  25.1 us
  transfers between devices with their start and end apart: 15, of which 15 were waited for; matrix products, arithmetic and copies ran while one was open for 11% of the time, Pallas kernels for 0%

profile of v2, /device:TPU:0, one launch (start us, length us, event | category | flops | bytes accessed | tf_op | source)
XLA Modules:
  0.0 771.0 jit_solution(440982275153732736)
XLA Ops:
  7.2 3.1 copy_bitcast_fusion
  13.2 8.3 %fusion = bf16[3072,3072]{1,0:T(8,128)(2,1)} fusion(s32[3072]{0:T(1024)S(1)} %bitcast.70), kind=kLoop, calls=%fused_computation.2 | loop fusion | flops 18874368 | bytes 18886656 | tf_op jit(solution)/shard_map/convert_element_type | solution.py:47
  22.1 1.6 copy-done.15
  23.9 2.0 slice-done
  25.8 16.7 %convolution_convert_fusion = bf16[592,3072]{1,0:T(8,128)(2,1)} fusion(bf16[3072,3072]{1,0:T(8,128)(2,1)} %fusion, bf16[16,3072]{1,0:T(8,128)(2,1)S(1)} %broadcast_in_dim.9, bf16[192,3072]{1,0:T(8,128)(2,1)S(1)} %get-tuple-element.22, bf16[192,3072]{1,0:T(8,128)(2,1)S(1)} %get-tuple-element.21, bf16[192,3072]{1,0:T(8,128)(2,1)S(1)} %slice-done), kind=kOutput, calls=%fused_computation.6 | convolution fusion | flops 11189993472 | bytes 26148864 | tf_op jit(solution)/shard_map/dot_general | solution.py:64
  42.5 5.2 fusion.45
  47.7 82.2 %all-gather.6.cloned.1.call-done = bf16[192,256,128]{2,0,1:T(8,128)(2,1)} async-done(((bf16[192,32,128]{2,0,1:T(8,128)(2,1)}), bf16[192,256,128]{2,0,1:T(8,128)(2,1)}) %all-gather.6.cloned.1.call-update) | async-done | bytes 12582928 | tf_op jit(solution)/shard_map/all_gather | solution.py:52
  130.0 7.2 gather_fusion
  137.2 3.4 multiply_bitcast_fusion
  140.5 5.8 fusion.28
  146.6 9.0 %convolution_convert_fusion.1 = bf16[192,3072]{1,0:T(8,128)(2,1)S(1)} fusion(bf16[192,3072]{1,0:T(8,128)(2,1)S(1)} %bitcast.68, bf16[3072,3072]{1,0:T(8,128)(2,1)} %fusion), kind=kOutput, calls=%fused_computation.11 | convolution fusion | flops 3624468480 | bytes 21233664 | tf_op jit(solution)/shard_map/dot_general | solution.py:80
  155.6 2.0 add_convert_fusion.3
  157.9 3.7 fusion.43
  161.6 2.0 add_convert_fusion.2
  163.6 26.6 %reduce-scatter.7.cloned.1.call-done = bf16[480,512]{1,0:T(8,128)(2,1)} async-done(((bf16[1920,512]{1,0:T(8,128)(2,1)}), bf16[480,512]{1,0:T(8,128)(2,1)}) %reduce-scatter.7.cloned.1.call-update) | async-done | bytes 491536 | tf_op jit(solution)/shard_map/reduce_scatter | solution.py:111
  190.3 15.8 %all_gather.22 = bf16[1024,256]{0,1:T(8,128)(2,1)S(1)} all-gather(bf16[256,256]{0,1:T(8,128)(2,1)S(1)} %pad.14), channel_id=1, replica_groups=mesh['dom'=8,'col'=4] {'col'}, dimensions={0}, use_global_device_ids=true | all-gather | bytes 655360 | tf_op jit(solution)/shard_map/all_gather | solution.py:58
  207.7 21.5 %reduce-scatter.9.cloned.1.call-done = bf16[480,512]{1,0:T(8,128)(2,1)} async-done(((bf16[1920,512]{1,0:T(8,128)(2,1)}), bf16[480,512]{1,0:T(8,128)(2,1)}) %reduce-scatter.9.cloned.1.call-update) | async-done | bytes 491536 | tf_op jit(solution)/shard_map/reduce_scatter | solution.py:111
  229.2 1.8 fusion.17
  233.7 34.3 %all-gather.8.cloned.1.call-done = bf16[1920,512]{1,0:T(8,128)(2,1)} async-done(((bf16[480,512]{1,0:T(8,128)(2,1)}), bf16[1920,512]{1,0:T(8,128)(2,1)}) %all-gather.8.cloned.1.call-update) | async-done | bytes 1966096 | tf_op jit(solution)/shard_map/all_gather | solution.py:129
  268.0 2.3 convolution_convert_fusion.7
  270.3 3.0 fusion.47
  276.2 55.5 %all-reduce.11.cloned.1.call-done = bf16[768,512]{1,0:T(8,128)(2,1)} async-done(((bf16[768,512]{1,0:T(8,128)(2,1)}), bf16[768,512]{1,0:T(8,128)(2,1)}) %all-reduce.11.cloned.1.call-update) | async-done | bytes 786448 | tf_op jit(solution)/shard_map/psum | solution.py:141
  333.1 33.8 %all-gather.10.cloned.1.call-done = bf16[1920,512]{1,0:T(8,128)(2,1)} async-done(((bf16[480,512]{1,0:T(8,128)(2,1)}), bf16[1920,512]{1,0:T(8,128)(2,1)}) %all-gather.10.cloned.1.call-update) | async-done | bytes 1966096 | tf_op jit(solution)/shard_map/all_gather | solution.py:129
  366.9 2.5 convolution_convert_fusion.6
  369.4 3.0 fusion.50
  373.4 21.4 %reduce-scatter.15.cloned.1.call-done = bf16[256,256]{0,1:T(8,128)(2,1)} async-done(((bf16[1024,256]{0,1:T(8,128)(2,1)}), bf16[256,256]{0,1:T(8,128)(2,1)}) %reduce-scatter.15.cloned.1.call-update) | async-done | bytes 131088 | tf_op jit(solution)/shard_map/reduce_scatter | solution.py:126
  394.9 3.8 fusion.37
  398.7 2.0 add_convert_fusion.1
  400.8 55.4 %all-reduce.17.cloned.1.call-done = (bf16[768,512]{1,0:T(8,128)(2,1)}, bf16[256,256]{0,1:T(8,128)(2,1)}) async-done(((bf16[768,512]{1,0:T(8,128)(2,1)}, bf16[256,256]{0,1:T(8,128)(2,1)}), (bf16[768,512]{1,0:T(8,128)(2,1)}, bf16[256,256]{0,1:T(8,128)(2,1)})) %all-reduce.17.cloned.1.call-update) | async-done | bytes 917520 | tf_op jit(solution)/shard_map/psum | solution.py:139
  457.5 4.3 fusion.35
  461.8 2.0 add_convert_fusion
  463.8 28.8 %reduce-scatter.11.cloned.1.call-done = bf16[480,512]{1,0:T(8,128)(2,1)} async-done(((bf16[1920,512]{1,0:T(8,128)(2,1)}), bf16[480,512]{1,0:T(8,128)(2,1)}) %reduce-scatter.11.cloned.1.call-update) | async-done | bytes 491536 | tf_op jit(solution)/shard_map/reduce_scatter | solution.py:111
  493.7 17.2 %all_gather.25 = bf16[1024,256]{0,1:T(8,128)(2,1)S(1)} all-gather(bf16[256,256]{0,1:T(8,128)(2,1)S(1)} %pad.16), channel_id=1, replica_groups=mesh['dom'=8,'col'=4] {'col'}, dimensions={0}, use_global_device_ids=true | all-gather | bytes 655360 | tf_op jit(solution)/shard_map/all_gather | solution.py:58
  510.9 21.8 %reduce-scatter.13.cloned.1.call-done = bf16[480,512]{1,0:T(8,128)(2,1)} async-done(((bf16[1920,512]{1,0:T(8,128)(2,1)}), bf16[480,512]{1,0:T(8,128)(2,1)}) %reduce-scatter.13.cloned.1.call-update) | async-done | bytes 491536 | tf_op jit(solution)/shard_map/reduce_scatter | solution.py:111
  532.6 1.8 fusion.24
  537.1 34.3 %all-gather.12.cloned.1.call-done = bf16[1920,512]{1,0:T(8,128)(2,1)} async-done(((bf16[480,512]{1,0:T(8,128)(2,1)}), bf16[1920,512]{1,0:T(8,128)(2,1)}) %all-gather.12.cloned.1.call-update) | async-done | bytes 1966096 | tf_op jit(solution)/shard_map/all_gather | solution.py:129
  571.5 2.5 convolution_convert_fusion.5
  574.0 3.0 fusion.53
  578.1 1.5 convolution_convert_fusion.2
  580.6 27.0 %all-gather.14.cloned.1.call-done = bf16[1920,512]{1,0:T(8,128)(2,1)} async-done(((bf16[480,512]{1,0:T(8,128)(2,1)}), bf16[1920,512]{1,0:T(8,128)(2,1)}) %all-gather.14.cloned.1.call-update) | async-done | bytes 1966096 | tf_op jit(solution)/shard_map/all_gather | solution.py:129
  607.6 2.5 convolution_convert_fusion.4
  610.1 3.0 fusion.56
  614.0 53.5 %all-reduce.13.cloned.1.call-done = bf16[768,512]{1,0:T(8,128)(2,1)} async-done(((bf16[768,512]{1,0:T(8,128)(2,1)}), bf16[768,512]{1,0:T(8,128)(2,1)}) %all-reduce.13.cloned.1.call-update) | async-done | bytes 786448 | tf_op jit(solution)/shard_map/psum | solution.py:141
  667.5 27.1 %reduce-scatter.17.cloned.1.call-done = bf16[256,256]{0,1:T(8,128)(2,1)} async-done(((bf16[1024,256]{0,1:T(8,128)(2,1)}), bf16[256,256]{0,1:T(8,128)(2,1)}) %reduce-scatter.17.cloned.1.call-update) | async-done | bytes 131088 | tf_op jit(solution)/shard_map/reduce_scatter | solution.py:126
  694.7 2.5 convert_element_type.240
  697.2 58.0 %all-reduce.15.cloned.1.call-done = (bf16[768,512]{1,0:T(8,128)(2,1)}, bf16[256,256]{0,1:T(8,128)(2,1)}) async-done(((bf16[768,512]{1,0:T(8,128)(2,1)}, bf16[256,256]{0,1:T(8,128)(2,1)}), (bf16[768,512]{1,0:T(8,128)(2,1)}, bf16[256,256]{0,1:T(8,128)(2,1)})) %all-reduce.15.cloned.1.call-update) | async-done | bytes 917520 | tf_op jit(solution)/shard_map/psum | solution.py:139
  758.7 2.2 fusion.60
  761.9 2.0 pad_maximum_fusion
  (145 shorter events, 25.3 us)
Async XLA Ops:
  7.2 130.0 %copy-start = (bf16[64,128,128]{2,1,0:T(8,128)(2,1)S(1)}, bf16[64,128,128]{2,1,0:T(8,128)(2,1)}, u32[]{:S(2)}) copy-start(bf16[64,128,128]{2,1,0:T(8,128)(2,1)} %param.12) | copy-start | bytes 6291460
  7.2 122.8 %all-gather.6.cloned.1.call-start = ((), (), s32[]{:S(2)}) async-start(), calls=%async_computation.6 | async-start | bytes 14155776 | tf_op jit(solution)/shard_map/all_gather | solution.py:52
  10.4 179.8 %reduce-scatter.7.cloned.1.call-start = ((), (), s32[]{:S(2)}) async-start(), calls=%async_computation.7 | async-start | bytes 2457600 | tf_op jit(solution)/shard_map/reduce_scatter | solution.py:111
  13.1 8.4 %copy-start.32 = (s32[64]{0:T(128)S(1)}, s32[64]{0:T(128)}, u32[]{:S(2)}) copy-start(s32[64]{0:T(128)} %param.14) | copy-start | bytes 772
  13.1 8.3 %copy-start.33 = (s32[64,1]{0,1:T(1,128)S(1)}, s32[64,1]{0,1:T(1,128)}, u32[]{:S(2)}) copy-start(s32[64,1]{0,1:T(1,128)} %param.13) | copy-start | bytes 772
  13.2 8.4 %copy-start.16 = (bf16[4,192,1024]{2,1,0:T(8,128)(2,1)S(1)}, bf16[4,192,1024]{2,1,0:T(8,128)(2,1)}, u32[]{:S(2)}) copy-start(bf16[4,192,1024]{2,1,0:T(8,128)(2,1)} %param.20) | copy-start | bytes 4718596
  21.8 1.9 copy-start.15
  23.7 18.8 %copy-start.2 = (f32[576,1024]{1,0:T(8,128)}, f32[576,1024]{1,0:T(8,128)S(1)}, u32[]{:S(2)}) copy-start(f32[576,1024]{1,0:T(8,128)S(1)} %maximum_convert_fusion) | copy-start | bytes 7077892
  23.7 2.2 slice-start
  137.2 3.4 copy-start.27
  146.6 9.0 %copy-start.17 = (bf16[24,8,24,128]{3,1,2,0:T(8,128)(2,1)}, bf16[24,8,24,128]{3,1,2,0:T(8,128)(2,1)S(1)}, u32[]{:S(2)}) copy-start(bf16[24,8,24,128]{3,1,2,0:T(8,128)(2,1)S(1)} %copy.26) | copy-start | bytes 3538948
  146.6 9.1 %copy-start.11 = (f32[1920,512]{1,0:T(8,128)S(1)}, f32[1920,512]{1,0:T(8,128)}, u32[]{:S(2)}) copy-start(f32[1920,512]{1,0:T(8,128)} %fusion.45) | copy-start | bytes 11796484
  155.6 112.4 %copy-start.7 = (bf16[192,3072]{1,0:T(8,128)(2,1)}, bf16[192,3072]{1,0:T(8,128)(2,1)S(1)}, u32[]{:S(2)}) copy-start(bf16[192,3072]{1,0:T(8,128)(2,1)S(1)} %convolution_convert_fusion.1) | copy-start | bytes 3538948
  157.7 71.5 %reduce-scatter.9.cloned.1.call-start = ((), (), s32[]{:S(2)}) async-start(), calls=%async_computation.8 | async-start | bytes 2457600 | tf_op jit(solution)/shard_map/reduce_scatter | solution.py:111
  163.6 26.6 %copy-start.18 = (bf16[256,153]{0,1:T(8,128)(2,1)S(1)}, bf16[256,153]{0,1:T(8,128)(2,1)}, u32[]{:S(2)}) copy-start(bf16[256,153]{0,1:T(8,128)(2,1)} %param.21) | copy-start | bytes 235012
  190.2 77.8 %all-gather.8.cloned.1.call-start = ((), (), s32[]{:S(2)}) async-start(), calls=%async_computation.9 | async-start | bytes 2457600 | tf_op jit(solution)/shard_map/all_gather | solution.py:129
  229.2 2.4 copy-start.19
  229.2 2.4 copy-start.20
  231.0 1.5 copy-start.13
  233.6 98.1 %all-reduce.11.cloned.1.call-start = ((), (), s32[]{:S(2)}) async-start(), calls=%async_computation.10 | async-start | bytes 1572864 | tf_op jit(solution)/shard_map/psum | solution.py:141
  268.0 2.3 copy-start.31
  273.3 1.6 copy-start.14
  274.3 92.6 %all-gather.10.cloned.1.call-start = ((), (), s32[]{:S(2)}) async-start(), calls=%async_computation.12 | async-start | bytes 2457600 | tf_op jit(solution)/shard_map/all_gather | solution.py:129
  274.9 119.9 %reduce-scatter.15.cloned.1.call-start = ((), (), s32[]{:S(2)}) async-start(), calls=%async_computation.14 | async-start | bytes 655360 | tf_op jit(solution)/shard_map/reduce_scatter | solution.py:126
  276.2 180.0 %all-reduce.17.cloned.1.call-start = ((), (), s32[]{:S(2)}) async-start(), calls=%async_computation.20 | async-start | bytes 1835008 | tf_op jit(solution)/shard_map/psum | solution.py:139
  333.1 423.6 %copy-start.4 = (f32[768,512]{1,0:T(8,128)}, f32[768,512]{1,0:T(8,128)S(1)}, u32[]{:S(2)}) copy-start(f32[768,512]{1,0:T(8,128)S(1)} %convert_element_type.218) | copy-start | bytes 4718596
  366.9 2.5 copy-start.29
  394.8 97.9 %reduce-scatter.11.cloned.1.call-start = ((), (), s32[]{:S(2)}) async-start(), calls=%async_computation.11 | async-start | bytes 2457600 | tf_op jit(solution)/shard_map/reduce_scatter | solution.py:111
  394.9 3.8 copy-start.8
  400.7 131.9 %reduce-scatter.13.cloned.1.call-start = ((), (), s32[]{:S(2)}) async-start(), calls=%async_computation.13 | async-start | bytes 2457600 | tf_op jit(solution)/shard_map/reduce_scatter | solution.py:111
  457.5 4.3 copy-start.5
  457.5 4.3 copy-start.9
  463.8 29.8 %copy-start.23 = (bf16[256,256]{0,1:T(8,128)(2,1)S(1)}, bf16[256,256]{0,1:T(8,128)(2,1)}, u32[]{:S(2)}) copy-start(bf16[256,256]{0,1:T(8,128)(2,1)} %get-tuple-element.18) | copy-start | bytes 393220
  492.7 78.8 %all-gather.12.cloned.1.call-start = ((), (), s32[]{:S(2)}) async-start(), calls=%async_computation.15 | async-start | bytes 2457600 | tf_op jit(solution)/shard_map/all_gather | solution.py:129
  532.6 2.4 copy-start.21
  532.6 2.4 copy-start.22
  534.5 1.5 copy-start.12
  537.1 70.5 %all-gather.14.cloned.1.call-start = ((), (), s32[]{:S(2)}) async-start(), calls=%async_computation.17 | async-start | bytes 2457600 | tf_op jit(solution)/shard_map/all_gather | solution.py:129
  571.5 96.0 %all-reduce.13.cloned.1.call-start = ((), (), s32[]{:S(2)}) async-start(), calls=%async_computation.16 | async-start | bytes 1572864 | tf_op jit(solution)/shard_map/psum | solution.py:141
  571.5 2.5 copy-start.30
  578.0 116.6 %reduce-scatter.17.cloned.1.call-start = ((), (), s32[]{:S(2)}) async-start(), calls=%async_computation.18 | async-start | bytes 655360 | tf_op jit(solution)/shard_map/reduce_scatter | solution.py:126
  580.5 174.6 %all-reduce.15.cloned.1.call-start = ((), (), s32[]{:S(2)}) async-start(), calls=%async_computation.19 | async-start | bytes 1835008 | tf_op jit(solution)/shard_map/psum | solution.py:139
  607.6 2.5 copy-start.28
  755.1 1.6 copy-start.6
  755.1 3.1 copy-start.10
  756.8 1.9 copy-start.3
  758.7 2.2 copy-start.24
  761.9 2.2 copy-start.1
  (2 other events, 1.5 us)
Sparse Core Ops, SparseCore 0:
  10.5 119.4 all-gather.5
  157.8 32.3 reduce-scatter.6
  193.8 35.3 reduce-scatter.8
  233.7 34.2 all-gather.7
  274.4 57.2 all-reduce.10
  333.6 33.2 all-gather.9
  370.0 24.7 reduce-scatter.14
  397.8 58.2 all-reduce.16
  459.5 33.1 reduce-scatter.10
  496.5 36.1 reduce-scatter.12
  537.2 34.2 all-gather.11
  573.3 34.2 all-gather.13
  610.0 57.4 all-reduce.12
  670.8 23.8 reduce-scatter.16
  697.1 58.0 all-reduce.14

commit v3 on v2

--- a/solution.py
+++ b/solution.py
@@ -4,7 +4,7 @@
 from jax.sharding import PartitionSpec as P
 
 STEPS = 2
-CHUNKS = 2
+CHUNKS = 1
 
 
 step_rate = 0.02

time: 776 us -> 593 us (0.76)
  waiting for transfers between devices: 582 us -> 410 us
  matrix products: 86.3 us -> 75.7 us
  blocking collectives: 33 us -> 42.9 us
    psum x2 -> x0, waiting for transfers between devices: 109 us -> none  [per_device(): both = lax.psum(both, 'dom')]
    reduce_scatter x4 -> x2, waiting for transfers between devices: 98.7 us -> 61.9 us  [per_device(): last = lax.psum_scatter(term, 'col', scatter_dimension=0, tiled=True)]
    all_gather x4 -> x2, waiting for transfers between devices: 129 us -> 98.6 us  [per_device(): lax.all_gather(after(dz[:, cuts[n]], last), 'col', axis=0, tiled=True)]
    psum x2, waiting for transfers between devices: 113 us -> 131 us  [per_device(): both, grad2 = lax.psum((both, grad2), 'dom')]
    reduce_scatter x2, waiting for transfers between devices: 48.6 us -> 36.5 us  [per_device(): grad2 = lax.psum_scatter(grad2, 'col', scatter_dimension=0, tiled=True)]
    all_gather x2, blocking collectives: 33 us -> 42.9 us  [whole_w2(): return lax.all_gather(low, 'col', axis=0, tiled=True)[:, :classes]]
    dot_general x8 -> x4, matrix products: 21.7 us -> 16 us  [per_device(): jnp.dot(x, last, preferred_element_type=jnp.float32).astype(jnp.bfloat16)]
    dot_general x8 -> x4, matrix products: 25.1 us -> 19.8 us  [rows_by(): jnp.einsum('dr,dj->rj', x, w.astype(jnp.bfloat16), preferred_element_type...]
  transfers between devices with their start and end apart: 15 -> 9, of which waited for: 15 -> 9; matrix products, arithmetic and copies ran while one was open for 11% -> 9% of each run, Pallas kernels for 0% -> 0%
where the time goes in v3:
time: 593 us; the launch traced here: 592 us
  waiting for transfers between devices  410 us (69%)
  matrix products  75.7 us (13%)
  blocking collectives  42.9 us (7%)
  other arithmetic  26.6 us (4%)
  local copies, waits for them, and re-layouts  21.3 us (4%)
  between operations  15 us (3%)
    psum x2, waiting for transfers between devices, per_device(): both, grad2 = lax.psum((both, grad2), 'dom')  131 us
    all_gather x2, waiting for transfers between devices, per_device(): lax.all_gather(after(dz[:, cuts[n]], last), 'col', axis=0, tiled=True)  98.6 us
    all_gather x1, waiting for transfers between devices, per_device(): piece = lax.all_gather(blocks, 'dom', axis=1, tiled=True)  82.3 us
    reduce_scatter x2, waiting for transfers between devices, per_device(): last = lax.psum_scatter(term, 'col', scatter_dimension=0, tiled=True)  61.9 us
    all_gather x2, blocking collectives, whole_w2(): return lax.all_gather(low, 'col', axis=0, tiled=True)[:, :classes]  42.9 us
    reduce_scatter x2, waiting for transfers between devices, per_device(): grad2 = lax.psum_scatter(grad2, 'col', scatter_dimension=0, tiled=True)  36.5 us
    dot_general x4, matrix products, rows_by(): jnp.einsum('dr,dj->rj', x, w.astype(jnp.bfloat16), preferred_element_type...  19.8 us
    dot_general x4, matrix products, per_device(): jnp.dot(x, last, preferred_element_type=jnp.float32).astype(jnp.bfloat16)  16 us
  transfers between devices with their start and end apart: 9, of which 9 were waited for; matrix products, arithmetic and copies ran while one was open for 9% of the time, Pallas kernels for 0%

profile of v3, /device:TPU:0, one launch (start us, length us, event | category | flops | bytes accessed | tf_op | source)
XLA Modules:
  0.0 592.1 jit_solution(1864112457889748932)
XLA Ops:
  7.2 3.1 copy_bitcast_fusion
  12.4 0.6 compare_select_fusion
  13.0 8.3 %fusion = bf16[3072,3072]{1,0:T(8,128)(2,1)} fusion(s32[3072]{0:T(1024)S(1)} %bitcast.73), kind=kLoop, calls=%fused_computation.2 | loop fusion | flops 18874368 | bytes 18886656 | tf_op jit(solution)/shard_map/convert_element_type | solution.py:47
  21.5 1.8 copy-done.5
  23.5 1.6 slice-done.2
  25.1 15.3 %convolution_convert_fusion = bf16[592,3072]{1,0:T(8,128)(2,1)S(1)} fusion(bf16[3072,3072]{1,0:T(8,128)(2,1)} %fusion, bf16[16,3072]{1,0:T(8,128)(2,1)S(1)} %broadcast_in_dim.9, bf16[192,3072]{1,0:T(8,128)(2,1)S(1)} %get-tuple-element.8, bf16[192,3072]{1,0:T(8,128)(2,1)S(1)} %get-tuple-element.7, bf16[192,3072]{1,0:T(8,128)(2,1)S(1)} %slice-done.2), kind=kOutput, calls=%fused_computation.8 | convolution fusion | flops 11189993472 | bytes 26148864 | tf_op jit(solution)/shard_map/dot_general | solution.py:64
  40.4 1.8 copy-done.23
  42.2 5.4 fusion.36
  47.7 82.3 %all-gather.4.cloned.1.call-done = bf16[192,256,128]{2,0,1:T(8,128)(2,1)} async-done(((bf16[192,32,128]{2,0,1:T(8,128)(2,1)}), bf16[192,256,128]{2,0,1:T(8,128)(2,1)}) %all-gather.4.cloned.1.call-update) | async-done | bytes 12582928 | tf_op jit(solution)/shard_map/all_gather | solution.py:52
  130.0 7.2 %gather_fusion = bf16[64,192,128]{2,1,0:T(8,128)(2,1)} fusion(bf16[192,256,128]{2,0,1:T(8,128)(2,1)} %all-gather.4.cloned.1.call-done, s32[1024]{0:T(1024)S(1)} %pad_clamp_fusion), kind=kCustom, calls=%fused_computation | custom fusion | bytes 6291712 | tf_op jit(solution)/shard_map/jit(_take)/gather | solution.py:70
  137.2 3.4 multiply_bitcast_fusion
  140.5 5.8 fusion.44
  146.6 9.1 %convolution_convert_fusion.1 = bf16[192,3072]{1,0:T(8,128)(2,1)S(1)} fusion(bf16[192,3072]{1,0:T(8,128)(2,1)S(1)} %bitcast.71, bf16[3072,3072]{1,0:T(8,128)(2,1)} %fusion), kind=kOutput, calls=%fused_computation.9 | convolution fusion | flops 3624468480 | bytes 21233664 | tf_op jit(solution)/shard_map/dot_general | solution.py:80
  155.8 4.1 add_convert_fusion.1
  160.0 0.8 copy-done.17
  160.8 22.4 %all_gather.16 = bf16[1024,256]{0,1:T(8,128)(2,1)S(1)} all-gather(bf16[256,256]{0,1:T(8,128)(2,1)S(1)} %pad.14), channel_id=1, replica_groups=mesh['dom'=8,'col'=4] {'col'}, dimensions={0}, use_global_device_ids=true | all-gather | bytes 655360 | tf_op jit(solution)/shard_map/all_gather | solution.py:58
  183.7 0.8 slice_convert_fusion
  184.6 29.7 %reduce-scatter.5.cloned.1.call-done = bf16[480,1024]{1,0:T(8,128)(2,1)} async-done(((bf16[1920,1024]{1,0:T(8,128)(2,1)}), bf16[480,1024]{1,0:T(8,128)(2,1)}) %reduce-scatter.5.cloned.1.call-update) | async-done | bytes 983056 | tf_op jit(solution)/shard_map/reduce_scatter | solution.py:111
  214.3 1.9 fusion.19
  216.7 1.9 fusion.22
  219.0 0.9 pad.15
  220.0 49.4 %all-gather.6.cloned.1.call-done = bf16[1920,1024]{1,0:T(8,128)(2,1)} async-done(((bf16[480,1024]{1,0:T(8,128)(2,1)}), bf16[1920,1024]{1,0:T(8,128)(2,1)}) %all-gather.6.cloned.1.call-update) | async-done | bytes 3932176 | tf_op jit(solution)/shard_map/all_gather | solution.py:129
  269.3 3.2 convolution_convert_fusion.3
  272.6 4.7 fusion.38
  277.3 1.3 pad_maximum_fusion.1
  278.6 18.2 %reduce-scatter.9.cloned.1.call-done = bf16[256,256]{0,1:T(8,128)(2,1)} async-done(((bf16[1024,256]{0,1:T(8,128)(2,1)}), bf16[256,256]{0,1:T(8,128)(2,1)}) %reduce-scatter.9.cloned.1.call-update) | async-done | bytes 131088 | tf_op jit(solution)/shard_map/reduce_scatter | solution.py:126
  296.9 65.6 %all-reduce.11.cloned.1.call-done = (bf16[768,1024]{1,0:T(8,128)(2,1)}, bf16[256,256]{0,1:T(8,128)(2,1)}) async-done(((bf16[768,1024]{1,0:T(8,128)(2,1)}, bf16[256,256]{0,1:T(8,128)(2,1)}), (bf16[768,1024]{1,0:T(8,128)(2,1)}, bf16[256,256]{0,1:T(8,128)(2,1)})) %all-reduce.11.cloned.1.call-update) | async-done | bytes 1703952 | tf_op jit(solution)/shard_map/psum | solution.py:139
  362.5 1.9 convert_element_type.168
  364.4 6.1 %fusion.32 = f32[1920,1024]{1,0:T(8,128)S(1)} fusion(bf16[592,3072]{1,0:T(8,128)(2,1)} %copy-done.23, f32[768,1024]{1,0:T(8,128)S(1)} %convert_element_type.168, bf16[192,1024]{1,0:T(8,128)(2,1)S(1)} %copy-done.11, bf16[192,1024]{1,0:T(8,128)(2,1)S(1)} %copy-done.9, bf16[192,1024]{1,0:T(8,128)(2,1)S(1)} %copy-done.7), kind=kOutput, calls=%fused_computation.46 | convolution fusion | flops 2270232576 | bytes 13615104 | tf_op jit(solution)/shard_map/dr,dj->rj/dot_general | solution.py:91
  370.6 4.2 add_convert_fusion
  375.7 20.5 %all_gather.18 = bf16[1024,256]{0,1:T(8,128)(2,1)} all-gather(bf16[256,256]{0,1:T(8,128)(2,1)S(1)} %pad.16), channel_id=1, replica_groups=mesh['dom'=8,'col'=4] {'col'}, dimensions={0}, use_global_device_ids=true | all-gather | bytes 655360 | tf_op jit(solution)/shard_map/all_gather | solution.py:58
  396.2 32.2 %reduce-scatter.7.cloned.1.call-done = bf16[480,1024]{1,0:T(8,128)(2,1)} async-done(((bf16[1920,1024]{1,0:T(8,128)(2,1)}), bf16[480,1024]{1,0:T(8,128)(2,1)}) %reduce-scatter.7.cloned.1.call-update) | async-done | bytes 983056 | tf_op jit(solution)/shard_map/reduce_scatter | solution.py:111
  428.4 1.9 fusion.26
  430.2 1.4 fusion.86
  431.8 1.9 fusion.29
  434.1 0.9 pad.17
  435.1 49.3 %all-gather.8.cloned.1.call-done = bf16[1920,1024]{1,0:T(8,128)(2,1)} async-done(((bf16[480,1024]{1,0:T(8,128)(2,1)}), bf16[1920,1024]{1,0:T(8,128)(2,1)}) %all-gather.8.cloned.1.call-update) | async-done | bytes 3932176 | tf_op jit(solution)/shard_map/all_gather | solution.py:129
  484.3 3.2 convolution_convert_fusion.2
  487.6 4.7 fusion.41
  492.4 1.3 pad_maximum_fusion.2
  493.7 18.3 %reduce-scatter.11.cloned.1.call-done = bf16[256,256]{0,1:T(8,128)(2,1)} async-done(((bf16[1024,256]{0,1:T(8,128)(2,1)}), bf16[256,256]{0,1:T(8,128)(2,1)}) %reduce-scatter.11.cloned.1.call-update) | async-done | bytes 131088 | tf_op jit(solution)/shard_map/reduce_scatter | solution.py:126
  512.0 65.2 %all-reduce.9.cloned.1.call-done = (bf16[768,1024]{1,0:T(8,128)(2,1)}, bf16[256,256]{0,1:T(8,128)(2,1)}) async-done(((bf16[768,1024]{1,0:T(8,128)(2,1)}, bf16[256,256]{0,1:T(8,128)(2,1)}), (bf16[768,1024]{1,0:T(8,128)(2,1)}, bf16[256,256]{0,1:T(8,128)(2,1)})) %all-reduce.9.cloned.1.call-update) | async-done | bytes 1703952 | tf_op jit(solution)/shard_map/psum | solution.py:139
  577.2 1.9 convert_element_type.185
  579.7 0.9 fusion.14
  580.5 1.3 fusion.51
  582.0 0.7 copy-done.19
  582.7 0.7 multiply_subtract_fusion
  583.4 2.0 pad_maximum_fusion
  (104 shorter events, 5.9 us)
Async XLA Ops:
  7.2 130.0 %copy-start = (bf16[64,128,128]{2,1,0:T(8,128)(2,1)S(1)}, bf16[64,128,128]{2,1,0:T(8,128)(2,1)}, u32[]{:S(2)}) copy-start(bf16[64,128,128]{2,1,0:T(8,128)(2,1)} %param.12) | copy-start | bytes 6291460
  7.2 122.8 %all-gather.4.cloned.1.call-start = ((), (), s32[]{:S(2)}) async-start(), calls=%async_computation.4 | async-start | bytes 14155776 | tf_op jit(solution)/shard_map/all_gather | solution.py:52
  10.4 0.7 copy-start.21
  10.4 0.7 copy-start.20
  10.4 203.9 %reduce-scatter.5.cloned.1.call-start = ((), (), s32[]{:S(2)}) async-start(), calls=%async_computation.5 | async-start | bytes 4915200 | tf_op jit(solution)/shard_map/reduce_scatter | solution.py:111
  13.0 8.4 %copy-start.26 = (s32[64]{0:T(128)S(1)}, s32[64]{0:T(128)}, u32[]{:S(2)}) copy-start(s32[64]{0:T(128)} %param.14) | copy-start | bytes 772
  13.0 8.4 %copy-start.27 = (s32[64,1]{0,1:T(1,128)S(1)}, s32[64,1]{0,1:T(1,128)}, u32[]{:S(2)}) copy-start(s32[64,1]{0,1:T(1,128)} %param.13) | copy-start | bytes 772
  13.0 8.4 %copy-start.4 = (bf16[4,192,1024]{2,1,0:T(8,128)(2,1)S(1)}, bf16[4,192,1024]{2,1,0:T(8,128)(2,1)}, u32[]{:S(2)}) copy-start(bf16[4,192,1024]{2,1,0:T(8,128)(2,1)} %param.20) | copy-start | bytes 4718596
  21.3 2.0 copy-start.5
  23.3 17.1 %copy-start.6 = (bf16[192,1024]{1,0:T(8,128)(2,1)}, bf16[192,1024]{1,0:T(8,128)(2,1)S(1)}, u32[]{:S(2)}) copy-start(bf16[192,1024]{1,0:T(8,128)(2,1)S(1)} %get-tuple-element.9) | copy-start | bytes 1179652
  23.3 17.1 %copy-start.8 = (bf16[192,1024]{1,0:T(8,128)(2,1)}, bf16[192,1024]{1,0:T(8,128)(2,1)S(1)}, u32[]{:S(2)}) copy-start(bf16[192,1024]{1,0:T(8,128)(2,1)S(1)} %get-tuple-element.10) | copy-start | bytes 1179652
  23.3 17.1 %copy-start.10 = (bf16[192,1024]{1,0:T(8,128)(2,1)}, bf16[192,1024]{1,0:T(8,128)(2,1)S(1)}, u32[]{:S(2)}) copy-start(bf16[192,1024]{1,0:T(8,128)(2,1)S(1)} %get-tuple-element.11) | copy-start | bytes 1179652
  23.3 1.8 slice-start.2
  40.4 1.8 copy-start.23
  137.2 3.4 copy-start.22
  146.4 9.4 %slice-start = ((s8[7864320]{0:T(1024)(128)(4,1)}), s8[4194304]{0:T(1024)(128)(4,1)S(1)}, s32[]{:S(2)}) async-start(s8[7864320]{0:T(1024)(128)(4,1)} %bitcast.67), calls=%async_computation.13 | async-start | bytes 8388608
  146.6 9.1 %copy-start.14 = (bf16[24,8,24,128]{3,1,2,0:T(8,128)(2,1)}, bf16[24,8,24,128]{3,1,2,0:T(8,128)(2,1)S(1)}, u32[]{:S(2)}) copy-start(bf16[24,8,24,128]{3,1,2,0:T(8,128)(2,1)S(1)} %copy.26) | copy-start | bytes 3538948
  146.6 9.1 %slice-start.1 = ((s8[7864320]{0:T(1024)(128)(4,1)}), s8[3670016]{0:T(1024)(128)(4,1)S(1)}, s32[]{:S(2)}) async-start(s8[7864320]{0:T(1024)(128)(4,1)} %bitcast.67), calls=%async_computation.14 | async-start | bytes 7340032
  159.9 0.9 copy-start.17
  159.9 109.4 %all-gather.6.cloned.1.call-start = ((), (), s32[]{:S(2)}) async-start(), calls=%async_computation.6 | async-start | bytes 4915200 | tf_op jit(solution)/shard_map/all_gather | solution.py:129
  214.3 2.4 copy-start.15
  218.6 78.2 %reduce-scatter.9.cloned.1.call-start = ((), (), s32[]{:S(2)}) async-start(), calls=%async_computation.8 | async-start | bytes 655360 | tf_op jit(solution)/shard_map/reduce_scatter | solution.py:126
  219.9 142.6 %all-reduce.11.cloned.1.call-start = ((), (), s32[]{:S(2)}) async-start(), calls=%async_computation.12 | async-start | bytes 3407872 | tf_op jit(solution)/shard_map/psum | solution.py:139
  269.3 3.3 copy-start.24
  296.8 131.5 %reduce-scatter.7.cloned.1.call-start = ((), (), s32[]{:S(2)}) async-start(), calls=%async_computation.7 | async-start | bytes 4915200 | tf_op jit(solution)/shard_map/reduce_scatter | solution.py:111
  362.5 1.9 copy-start.7
  362.5 1.9 copy-start.9
  362.5 1.9 copy-start.11
  364.4 6.1 %copy-start.2 = (f32[768,1024]{1,0:T(8,128)}, f32[768,1024]{1,0:T(8,128)S(1)}, u32[]{:S(2)}) copy-start(f32[768,1024]{1,0:T(8,128)S(1)} %convert_element_type.168) | copy-start | bytes 9437188
  374.7 0.9 copy-start.18
  374.8 109.6 %all-gather.8.cloned.1.call-start = ((), (), s32[]{:S(2)}) async-start(), calls=%async_computation.9 | async-start | bytes 4915200 | tf_op jit(solution)/shard_map/all_gather | solution.py:129
  428.3 3.4 copy-start.13
  428.3 3.4 copy-start.16
  433.7 78.3 %reduce-scatter.11.cloned.1.call-start = ((), (), s32[]{:S(2)}) async-start(), calls=%async_computation.10 | async-start | bytes 655360 | tf_op jit(solution)/shard_map/reduce_scatter | solution.py:126
  435.0 142.2 %all-reduce.9.cloned.1.call-start = ((), (), s32[]{:S(2)}) async-start(), calls=%async_computation.11 | async-start | bytes 3407872 | tf_op jit(solution)/shard_map/psum | solution.py:139
  484.3 3.3 copy-start.25
  577.2 2.4 copy-start.3
  577.2 2.4 copy-start.12
  581.8 0.9 copy-start.19
  583.4 2.2 copy-start.1
Sparse Core Ops, SparseCore 0:
  10.5 119.4 all-gather.3
  160.0 54.2 reduce-scatter.4
  218.8 50.5 all-gather.5
  272.0 24.7 reduce-scatter.8
  299.8 62.6 all-reduce.10
  374.9 53.4 reduce-scatter.6
  433.8 50.4 all-gather.7
  487.2 24.7 reduce-scatter.10
  514.6 62.6 all-reduce.8

commit v4 on v3

--- a/solution.py
+++ b/solution.py
@@ -123,7 +123,14 @@
         dz = (back * sig * (1.0 + z * (1.0 - sig))).astype(jnp.bfloat16)
         grad2 = jnp.dot(hidden.T, slope, preferred_element_type=jnp.float32)
         grad2 = jnp.pad(grad2.astype(jnp.bfloat16), ((0, 0), (0, wide - classes)))
-        grad2 = lax.psum_scatter(grad2, "col", scatter_dimension=0, tiled=True)
+        own = hid // ncol
+        parts = []
+        for k in range(ncol):
+            part = lax.dynamic_slice_in_dim(grad2, (col + k) % ncol * own, own, axis=0)
+            if k:
+                part = lax.ppermute(part, "col", [(c, (c + k) % ncol) for c in range(ncol)])
+            parts.append(part.astype(jnp.float32))
+        grad2 = sum(parts).astype(jnp.bfloat16)
         last, last_sum = None, None
         for n in range(CHUNKS):
             last = lax.all_gather(after(dz[:, cuts[n]], last), "col", axis=0, tiled=True)

time: 593 us -> 550 us (0.927)
  waiting for transfers between devices: 410 us -> 359 us
  starting transfers between devices: 0.37 us -> 8.98 us
    reduce_scatter x2 -> x0, waiting for transfers between devices: 36.5 us -> none  [per_device(): grad2 = lax.psum_scatter(grad2, 'col', scatter_dimension=0, tiled=True)]
    all_gather x2, waiting for transfers between devices: 98.6 us -> 80 us  [per_device(): lax.all_gather(after(dz[:, cuts[n]], last), 'col', axis=0, tiled=True)]
    ppermute x0 -> x6, waiting for transfers between devices: none -> 9.28 us  [per_device(): part = lax.ppermute(part, 'col', [(c, (c + k) % ncol) for c in range(ncol)])]
    ppermute x0 -> x6, starting transfers between devices: none -> 8.69 us  [per_device(): part = lax.ppermute(part, 'col', [(c, (c + k) % ncol) for c in range(ncol)])]
  transfers between devices with their start and end apart: 9 -> 13, of which waited for: 9 -> 11; matrix products, arithmetic and copies ran while one was open for 9% -> 7% of each run, Pallas kernels for 0% -> 0%
where the time goes in v4:
time: 550 us; the launch traced here: 549 us
  waiting for transfers between devices  359 us (65%)
  matrix products  75.3 us (14%)
  blocking collectives  42.9 us (8%)
  other arithmetic  28 us (5%)
  local copies, waits for them, and re-layouts  19.6 us (4%)
  between operations  15.4 us (3%)
  starting transfers between devices  8.98 us (2%)
    psum x2, waiting for transfers between devices, per_device(): both, grad2 = lax.psum((both, grad2), 'dom')  126 us
    all_gather x1, waiting for transfers between devices, per_device(): piece = lax.all_gather(blocks, 'dom', axis=1, tiled=True)  82.3 us
    all_gather x2, waiting for transfers between devices, per_device(): lax.all_gather(after(dz[:, cuts[n]], last), 'col', axis=0, tiled=True)  80 us
    reduce_scatter x2, waiting for transfers between devices, per_device(): last = lax.psum_scatter(term, 'col', scatter_dimension=0, tiled=True)  61.9 us
    all_gather x2, blocking collectives, whole_w2(): return lax.all_gather(low, 'col', axis=0, tiled=True)[:, :classes]  42.9 us
    dot_general x4, matrix products, rows_by(): jnp.einsum('dr,dj->rj', x, w.astype(jnp.bfloat16), preferred_element_type...  19.8 us
    dot_general x1, matrix products, per_device(): jnp.dot(known, moves, preferred_element_type=jnp.float32)  15.3 us
    dot_general x4, matrix products, per_device(): jnp.dot(x, last, preferred_element_type=jnp.float32).astype(jnp.bfloat16)  14.6 us
  transfers between devices with their start and end apart: 13, of which 11 were waited for; matrix products, arithmetic and copies ran while one was open for 7% of the time, Pallas kernels for 0%

profile of v4, /device:TPU:0, one launch (start us, length us, event | category | flops | bytes accessed | tf_op | source)
XLA Modules:
  0.0 549.2 jit_solution(16399524179254334137)
XLA Ops:
  7.2 3.1 copy_bitcast_fusion
  13.0 8.3 %fusion = bf16[3072,3072]{1,0:T(8,128)(2,1)} fusion(s32[3072]{0:T(1024)S(1)} %bitcast.73), kind=kLoop, calls=%fused_computation.2 | loop fusion | flops 18874368 | bytes 18886656 | tf_op jit(solution)/shard_map/convert_element_type | solution.py:47
  21.5 1.8 copy-done.5
  23.5 1.6 slice-done.2
  25.1 15.3 %convolution_convert_fusion = bf16[592,3072]{1,0:T(8,128)(2,1)S(1)} fusion(bf16[3072,3072]{1,0:T(8,128)(2,1)} %fusion, bf16[16,3072]{1,0:T(8,128)(2,1)S(1)} %broadcast_in_dim.9, bf16[192,3072]{1,0:T(8,128)(2,1)S(1)} %get-tuple-element.8, bf16[192,3072]{1,0:T(8,128)(2,1)S(1)} %get-tuple-element.7, bf16[192,3072]{1,0:T(8,128)(2,1)S(1)} %slice-done.2), kind=kOutput, calls=%fused_computation.8 | convolution fusion | flops 11189993472 | bytes 26148864 | tf_op jit(solution)/shard_map/dot_general | solution.py:64
  40.4 1.8 copy-done.24
  42.2 5.5 fusion.36
  47.7 82.3 %all-gather.4.cloned.1.call-done = bf16[192,256,128]{2,0,1:T(8,128)(2,1)} async-done(((bf16[192,32,128]{2,0,1:T(8,128)(2,1)}), bf16[192,256,128]{2,0,1:T(8,128)(2,1)}) %all-gather.4.cloned.1.call-update) | async-done | bytes 12582928 | tf_op jit(solution)/shard_map/all_gather | solution.py:52
  130.0 7.2 %gather_fusion = bf16[64,192,128]{2,1,0:T(8,128)(2,1)} fusion(bf16[192,256,128]{2,0,1:T(8,128)(2,1)} %all-gather.4.cloned.1.call-done, s32[1024]{0:T(1024)S(1)} %pad_clamp_fusion), kind=kCustom, calls=%fused_computation | custom fusion | bytes 6291712 | tf_op jit(solution)/shard_map/jit(_take)/gather | solution.py:70
  137.2 3.4 multiply_bitcast_fusion
  140.5 5.8 %fusion.44 = bf16[24,192,128]{2,0,1:T(8,128)(2,1)S(1)} fusion(f32[192,64,128]{2,0,1:T(8,128)S(1)} %multiply_bitcast_fusion, s32[64]{0:T(128)S(1)} %copy-done.23), kind=kOutput, calls=%fused_computation.57 | convolution fusion | flops 453576192 | bytes 7471360 | tf_op jit(solution)/shard_map/dti,tb->dbi/dot_general | solution.py:78
  146.6 9.1 %convolution_convert_fusion.1 = bf16[192,3072]{1,0:T(8,128)(2,1)S(1)} fusion(bf16[192,3072]{1,0:T(8,128)(2,1)S(1)} %bitcast.71, bf16[3072,3072]{1,0:T(8,128)(2,1)} %fusion), kind=kOutput, calls=%fused_computation.9 | convolution fusion | flops 3624468480 | bytes 21233664 | tf_op jit(solution)/shard_map/dot_general | solution.py:80
  155.8 4.1 add_convert_fusion.1
  160.7 22.4 %all_gather.16 = bf16[1024,256]{0,1:T(8,128)(2,1)S(1)} all-gather(bf16[256,256]{0,1:T(8,128)(2,1)S(1)} %pad.14), channel_id=1, replica_groups=mesh['dom'=8,'col'=4] {'col'}, dimensions={0}, use_global_device_ids=true | all-gather | bytes 655360 | tf_op jit(solution)/shard_map/all_gather | solution.py:58
  184.6 29.7 %reduce-scatter.3.cloned.1.call-done = bf16[480,1024]{1,0:T(8,128)(2,1)} async-done(((bf16[1920,1024]{1,0:T(8,128)(2,1)}), bf16[480,1024]{1,0:T(8,128)(2,1)}) %reduce-scatter.3.cloned.1.call-update) | async-done | bytes 983056 | tf_op jit(solution)/shard_map/reduce_scatter | solution.py:111
  214.3 1.9 fusion.19
  216.7 1.9 fusion.22
  219.1 1.4 collective-permute-start
  221.2 2.3 collective-permute-start.2
  223.5 3.0 collective-permute-done
  226.4 1.7 collective-permute-done.1
  228.8 40.5 %all-gather.6.cloned.1.call-done = bf16[1920,1024]{1,0:T(8,128)(2,1)} async-done(((bf16[480,1024]{1,0:T(8,128)(2,1)}), bf16[1920,1024]{1,0:T(8,128)(2,1)}) %all-gather.6.cloned.1.call-update) | async-done | bytes 3932176 | tf_op jit(solution)/shard_map/all_gather | solution.py:136
  269.3 3.2 convolution_convert_fusion.3
  272.6 4.7 fusion.38
  277.3 1.3 pad_maximum_fusion.1
  278.6 62.8 %all-reduce.11.cloned.1.call-done = (bf16[768,1024]{1,0:T(8,128)(2,1)}, bf16[256,256]{0,1:T(8,128)(2,1)}) async-done(((bf16[768,1024]{1,0:T(8,128)(2,1)}, bf16[256,256]{0,1:T(8,128)(2,1)}), (bf16[768,1024]{1,0:T(8,128)(2,1)}, bf16[256,256]{0,1:T(8,128)(2,1)})) %all-reduce.11.cloned.1.call-update) | async-done | bytes 1703952 | tf_op jit(solution)/shard_map/psum | solution.py:146
  341.4 1.9 convert_element_type.198
  343.3 6.1 %fusion.32 = f32[1920,1024]{1,0:T(8,128)S(1)} fusion(bf16[592,3072]{1,0:T(8,128)(2,1)} %copy-done.24, f32[768,1024]{1,0:T(8,128)S(1)} %convert_element_type.198, bf16[192,1024]{1,0:T(8,128)(2,1)S(1)} %copy-done.11, bf16[192,1024]{1,0:T(8,128)(2,1)S(1)} %copy-done.9, bf16[192,1024]{1,0:T(8,128)(2,1)S(1)} %copy-done.7), kind=kOutput, calls=%fused_computation.46 | convolution fusion | flops 2270232576 | bytes 13615104 | tf_op jit(solution)/shard_map/dr,dj->rj/dot_general | solution.py:91
  349.5 4.1 add_convert_fusion
  354.6 20.5 %all_gather.18 = bf16[1024,256]{0,1:T(8,128)(2,1)} all-gather(bf16[256,256]{0,1:T(8,128)(2,1)S(1)} %pad.16), channel_id=1, replica_groups=mesh['dom'=8,'col'=4] {'col'}, dimensions={0}, use_global_device_ids=true | all-gather | bytes 655360 | tf_op jit(solution)/shard_map/all_gather | solution.py:58
  375.0 32.2 %reduce-scatter.5.cloned.1.call-done = bf16[480,1024]{1,0:T(8,128)(2,1)} async-done(((bf16[1920,1024]{1,0:T(8,128)(2,1)}), bf16[480,1024]{1,0:T(8,128)(2,1)}) %reduce-scatter.5.cloned.1.call-update) | async-done | bytes 983056 | tf_op jit(solution)/shard_map/reduce_scatter | solution.py:111
  407.3 1.9 fusion.26
  409.1 1.4 fusion.86
  410.7 1.9 fusion.29
  412.7 1.3 convolution_convert_fusion.4
  414.0 1.4 collective-permute-start.3
  416.1 2.3 collective-permute-start.5
  418.4 3.0 collective-permute-done.3
  421.4 1.6 collective-permute-done.4
  423.7 39.5 %all-gather.8.cloned.1.call-done = bf16[1920,1024]{1,0:T(8,128)(2,1)} async-done(((bf16[480,1024]{1,0:T(8,128)(2,1)}), bf16[1920,1024]{1,0:T(8,128)(2,1)}) %all-gather.8.cloned.1.call-update) | async-done | bytes 3932176 | tf_op jit(solution)/shard_map/all_gather | solution.py:136
  463.3 5.5 %fusion.41 = bf16[576,1024]{1,0:T(8,128)(2,1)S(1)} fusion(bf16[1920,1024]{1,0:T(8,128)(2,1)} %all-gather.8.cloned.1.call-done, bf16[592,3072]{1,0:T(8,128)(2,1)} %copy-done.24), kind=kOutput, calls=%fused_computation.56 | convolution fusion | flops 2265513984 | bytes 7323648 | tf_op jit(solution)/shard_map/dot_general | solution.py:139
  468.8 1.0 convolution_convert_fusion.2
  469.9 1.3 pad_maximum_fusion.2
  471.2 62.8 %all-reduce.9.cloned.1.call-done = (bf16[768,1024]{1,0:T(8,128)(2,1)}, bf16[256,256]{0,1:T(8,128)(2,1)}) async-done(((bf16[768,1024]{1,0:T(8,128)(2,1)}, bf16[256,256]{0,1:T(8,128)(2,1)}), (bf16[768,1024]{1,0:T(8,128)(2,1)}, bf16[256,256]{0,1:T(8,128)(2,1)})) %all-reduce.9.cloned.1.call-update) | async-done | bytes 1703952 | tf_op jit(solution)/shard_map/psum | solution.py:146
  534.0 1.9 convert_element_type.220
  536.4 0.9 fusion.14
  537.3 1.3 fusion.51
  540.2 2.0 pad_maximum_fusion
  (114 shorter events, 12.0 us)
Async XLA Ops:
  7.2 130.0 %copy-start = (bf16[64,128,128]{2,1,0:T(8,128)(2,1)S(1)}, bf16[64,128,128]{2,1,0:T(8,128)(2,1)}, u32[]{:S(2)}) copy-start(bf16[64,128,128]{2,1,0:T(8,128)(2,1)} %param.12) | copy-start | bytes 6291460
  7.2 122.8 %all-gather.4.cloned.1.call-start = ((), (), s32[]{:S(2)}) async-start(), calls=%async_computation.2 | async-start | bytes 14155776 | tf_op jit(solution)/shard_map/all_gather | solution.py:52
  10.4 0.7 copy-start.22
  10.4 0.7 copy-start.21
  10.4 203.9 %reduce-scatter.3.cloned.1.call-start = ((), (), s32[]{:S(2)}) async-start(), calls=%async_computation.3 | async-start | bytes 4915200 | tf_op jit(solution)/shard_map/reduce_scatter | solution.py:111
  13.0 8.4 %copy-start.27 = (s32[64]{0:T(128)S(1)}, s32[64]{0:T(128)}, u32[]{:S(2)}) copy-start(s32[64]{0:T(128)} %param.14) | copy-start | bytes 772
  13.0 8.3 %copy-start.28 = (s32[64,1]{0,1:T(1,128)S(1)}, s32[64,1]{0,1:T(1,128)}, u32[]{:S(2)}) copy-start(s32[64,1]{0,1:T(1,128)} %param.13) | copy-start | bytes 772
  13.0 8.4 %copy-start.4 = (bf16[4,192,1024]{2,1,0:T(8,128)(2,1)S(1)}, bf16[4,192,1024]{2,1,0:T(8,128)(2,1)}, u32[]{:S(2)}) copy-start(bf16[4,192,1024]{2,1,0:T(8,128)(2,1)} %param.20) | copy-start | bytes 4718596
  21.3 2.0 copy-start.5
  23.3 17.1 %copy-start.6 = (bf16[192,1024]{1,0:T(8,128)(2,1)}, bf16[192,1024]{1,0:T(8,128)(2,1)S(1)}, u32[]{:S(2)}) copy-start(bf16[192,1024]{1,0:T(8,128)(2,1)S(1)} %get-tuple-element.9) | copy-start | bytes 1179652
  23.3 17.1 %copy-start.8 = (bf16[192,1024]{1,0:T(8,128)(2,1)}, bf16[192,1024]{1,0:T(8,128)(2,1)S(1)}, u32[]{:S(2)}) copy-start(bf16[192,1024]{1,0:T(8,128)(2,1)S(1)} %get-tuple-element.10) | copy-start | bytes 1179652
  23.3 17.1 %copy-start.10 = (bf16[192,1024]{1,0:T(8,128)(2,1)}, bf16[192,1024]{1,0:T(8,128)(2,1)S(1)}, u32[]{:S(2)}) copy-start(bf16[192,1024]{1,0:T(8,128)(2,1)S(1)} %get-tuple-element.11) | copy-start | bytes 1179652
  23.3 1.8 slice-start.2
  40.4 1.8 copy-start.24
  137.2 3.4 copy-start.23
  146.4 9.4 %slice-start = ((s8[7864320]{0:T(1024)(128)(4,1)}), s8[4194304]{0:T(1024)(128)(4,1)S(1)}, s32[]{:S(2)}) async-start(s8[7864320]{0:T(1024)(128)(4,1)} %bitcast.67), calls=%async_computation.9 | async-start | bytes 8388608
  146.6 9.1 %copy-start.15 = (bf16[24,8,24,128]{3,1,2,0:T(8,128)(2,1)}, bf16[24,8,24,128]{3,1,2,0:T(8,128)(2,1)S(1)}, u32[]{:S(2)}) copy-start(bf16[24,8,24,128]{3,1,2,0:T(8,128)(2,1)S(1)} %copy.26) | copy-start | bytes 3538948
  146.6 9.1 %slice-start.1 = ((s8[7864320]{0:T(1024)(128)(4,1)}), s8[3670016]{0:T(1024)(128)(4,1)S(1)}, s32[]{:S(2)}) async-start(s8[7864320]{0:T(1024)(128)(4,1)} %bitcast.67), calls=%async_computation.10 | async-start | bytes 7340032
  159.8 0.9 copy-start.18
  159.9 109.4 %all-gather.6.cloned.1.call-start = ((), (), s32[]{:S(2)}) async-start(), calls=%async_computation.4 | async-start | bytes 4915200 | tf_op jit(solution)/shard_map/all_gather | solution.py:136
  214.3 2.4 copy-start.16
  218.6 122.8 %all-reduce.11.cloned.1.call-start = ((), (), s32[]{:S(2)}) async-start(), calls=%async_computation.8 | async-start | bytes 3407872 | tf_op jit(solution)/shard_map/psum | solution.py:146
  219.1 7.3 %collective-permute-start = (bf16[256,256]{0,1:T(8,128)(2,1)S(1)}, bf16[256,256]{0,1:T(8,128)(2,1)S(1)}, u32[]{:S(2)}, u32[]{:S(2)}) collective-permute-start(bf16[256,256]{0,1:T(8,128)(2,1)S(1)} %get-tuple-element.15), channel_id=1, source_target_pairs={{0,1},{1,2},{2,3},{3,0},{4,5},{5,6},{6,7},{7,4},{8,9},{9,10},{10,1... | collective-permute-start | bytes 393224 | tf_op jit(solution)/shard_map/ppermute | solution.py:131
  220.5 7.6 %collective-permute-start.1 = (bf16[256,256]{0,1:T(8,128)(2,1)S(1)}, bf16[256,256]{0,1:T(8,128)(2,1)S(1)}, u32[]{:S(2)}, u32[]{:S(2)}) collective-permute-start(bf16[256,256]{0,1:T(8,128)(2,1)S(1)} %get-tuple-element.16), channel_id=1, source_target_pairs={{0,2},{1,3},{2,0},{3,1},{4,6},{5,7},{6,4},{7,5},{8,10},{9,11},{10,... | collective-permute-start | bytes 393224 | tf_op jit(solution)/shard_map/ppermute | solution.py:131
  221.2 6.9 %collective-permute-start.2 = (bf16[256,256]{0,1:T(8,128)(2,1)S(1)}, bf16[256,256]{0,1:T(8,128)(2,1)S(1)}, u32[]{:S(2)}, u32[]{:S(2)}) collective-permute-start(bf16[256,256]{0,1:T(8,128)(2,1)S(1)} %get-tuple-element.17), channel_id=1, source_target_pairs={{0,3},{1,0},{2,1},{3,2},{4,7},{5,4},{6,5},{7,6},{8,11},{9,8},{10,9... | collective-permute-start | bytes 393224 | tf_op jit(solution)/shard_map/ppermute | solution.py:131
  269.3 3.3 copy-start.25
  278.6 128.6 %reduce-scatter.5.cloned.1.call-start = ((), (), s32[]{:S(2)}) async-start(), calls=%async_computation.5 | async-start | bytes 4915200 | tf_op jit(solution)/shard_map/reduce_scatter | solution.py:111
  341.4 1.9 copy-start.7
  341.4 1.9 copy-start.9
  341.4 1.9 copy-start.11
  343.3 6.1 %copy-start.2 = (f32[768,1024]{1,0:T(8,128)}, f32[768,1024]{1,0:T(8,128)S(1)}, u32[]{:S(2)}) copy-start(f32[768,1024]{1,0:T(8,128)S(1)} %convert_element_type.198) | copy-start | bytes 9437188
  353.6 0.9 copy-start.19
  353.6 109.6 %all-gather.8.cloned.1.call-start = ((), (), s32[]{:S(2)}) async-start(), calls=%async_computation.6 | async-start | bytes 4915200 | tf_op jit(solution)/shard_map/all_gather | solution.py:136
  407.2 3.4 copy-start.13
  407.2 3.4 copy-start.17
  410.6 2.0 copy-start.14
  412.6 121.4 %all-reduce.9.cloned.1.call-start = ((), (), s32[]{:S(2)}) async-start(), calls=%async_computation.7 | async-start | bytes 3407872 | tf_op jit(solution)/shard_map/psum | solution.py:146
  414.0 7.3 %collective-permute-start.3 = (bf16[256,256]{0,1:T(8,128)(2,1)S(1)}, bf16[256,256]{0,1:T(8,128)(2,1)S(1)}, u32[]{:S(2)}, u32[]{:S(2)}) collective-permute-start(bf16[256,256]{0,1:T(8,128)(2,1)S(1)} %get-tuple-element.12), channel_id=1, source_target_pairs={{0,1},{1,2},{2,3},{3,0},{4,5},{5,6},{6,7},{7,4},{8,9},{9,10},{10,1... | collective-permute-start | bytes 393224 | tf_op jit(solution)/shard_map/ppermute | solution.py:131
  415.4 7.6 %collective-permute-start.4 = (bf16[256,256]{0,1:T(8,128)(2,1)S(1)}, bf16[256,256]{0,1:T(8,128)(2,1)S(1)}, u32[]{:S(2)}, u32[]{:S(2)}) collective-permute-start(bf16[256,256]{0,1:T(8,128)(2,1)S(1)} %get-tuple-element.13), channel_id=1, source_target_pairs={{0,2},{1,3},{2,0},{3,1},{4,6},{5,7},{6,4},{7,5},{8,10},{9,11},{10,... | collective-permute-start | bytes 393224 | tf_op jit(solution)/shard_map/ppermute | solution.py:131
  416.1 6.9 %collective-permute-start.5 = (bf16[256,256]{0,1:T(8,128)(2,1)S(1)}, bf16[256,256]{0,1:T(8,128)(2,1)S(1)}, u32[]{:S(2)}, u32[]{:S(2)}) collective-permute-start(bf16[256,256]{0,1:T(8,128)(2,1)S(1)} %get-tuple-element.14), channel_id=1, source_target_pairs={{0,3},{1,0},{2,1},{3,2},{4,7},{5,4},{6,5},{7,6},{8,11},{9,8},{10,9... | collective-permute-start | bytes 393224 | tf_op jit(solution)/shard_map/ppermute | solution.py:131
  463.3 5.5 %copy-start.26 = (bf16[1920,1024]{1,0:T(8,128)(2,1)S(1)}, bf16[1920,1024]{1,0:T(8,128)(2,1)}, u32[]{:S(2)}) copy-start(bf16[1920,1024]{1,0:T(8,128)(2,1)} %all-gather.8.cloned.1.call-done) | copy-start | bytes 11796484
  534.0 2.4 copy-start.3
  534.0 2.4 copy-start.12
  538.6 0.9 copy-start.20
  540.2 2.2 copy-start.1
Sparse Core Ops, SparseCore 0:
  10.5 119.4 all-gather.3
  160.0 54.2 reduce-scatter.2
  218.7 50.5 all-gather.5
  278.7 62.6 all-reduce.10
  353.8 53.4 reduce-scatter.4
  412.7 50.5 all-gather.7
  471.3 62.6 all-reduce.8
